TPU v7x, 32 devices: a whole 2x2x4 slice. The times are simulated.
32 devices in a mesh: grp: 2 (over y), pair: 4 (over z), rep: 2 (over x), sub: 2 (over core).
Axes of the slice: x: 2, y: 2, z: 4, core: 2. Of those that a mesh axis runs over, the one named last changes fastest.
Arguments:
- cholesky: bfloat16 [256, 640, 640], P('sub', 'pair'), may hold values from -0.015625 to 0.015625
- trial_orbitals: bfloat16 [640, 192], replicated, may hold values from -0.25 to 0.25
- walkers: bfloat16 [32, 640, 192], P(('grp', 'pair', 'rep'), None, 'sub'), parts along dimension 0, may hold values from -6 to 6
- intersection_inverse: bfloat16 [32, 192, 192], P(('grp', 'pair', 'rep')), parts along dimension 0, may hold values from -0.4375 to 0.4375
- noise_stream: float32 [2048], P('grp'), parts along dimension 0, may hold values from -6 to 6
- offsets: int32 [32], P('grp'), parts along dimension 0, may hold values from 0 to 768
- parents: int32 [32], P(('grp', 'pair', 'rep')), parts along dimension 0, may hold values from 0 to 7
Outputs:
- new_walkers: bfloat16 [32, 640, 192], P(('grp', 'pair', 'rep'), None, 'sub'), parts along dimension 0
- force_bias: float32 [32, 256], P(('grp', 'pair', 'rep'), 'sub'), parts along dimension 0
There are 2 independent parts, one for each index of `grp`. A program takes and returns all parts, laid end to end along the dimension named above; an argument that names none is the same for every part. Nothing has to cross between parts.
All inputs are finite; a program needn't handle non-finite values.
Results may differ from a plain program's by a relative error of at most 0.035.
Values may be sent and summed in bfloat16 or wider, within the bound.
A program may use at most 64 MiB of HBM per device.

v0:
```python
import jax
import jax.numpy as jnp
from jax import lax
from jax.sharding import PartitionSpec as P

TAYLOR = 6


field_scale = 1.6


def shards(cholesky, trial_orbitals, walkers, intersection_inverse, noise_stream, offsets, parents):
    chol_count = cholesky.shape[0]
    walk_count = walkers.shape[0]
    pair_size = lax.axis_size("pair")
    rep_size = lax.axis_size("rep")
    pair_index = lax.axis_index("pair")
    rep_index = lax.axis_index("rep")
    sub_index = lax.axis_index("sub")
    half_rotated = jnp.einsum(
        "gpq,qi->gpi", cholesky, trial_orbitals, preferred_element_type=jnp.float32
    ).astype(jnp.bfloat16)
    whole_walkers = lax.all_gather(walkers, "sub", axis=2, tiled=True)
    mixed = jnp.einsum(
        "wpj,wji->wpi", whole_walkers, intersection_inverse, preferred_element_type=jnp.float32
    ).astype(jnp.bfloat16)
    mixed_rows = lax.all_to_all(mixed, "pair", split_axis=1, concat_axis=0, tiled=True)
    partial_bias = jnp.einsum(
        "jpi,gpi->jg", mixed_rows, half_rotated, preferred_element_type=jnp.float32
    )
    window_start = sub_index * chol_count
    vector_steps = jnp.arange(chol_count, dtype=jnp.int32)

    def window_fields(offset_value, bias_row):
        drawn = noise_stream[offset_value + window_start + vector_steps]
        return (drawn - bias_row).astype(jnp.bfloat16)

    offsets_grid = offsets.reshape(pair_size, rep_size, walk_count)
    bias_totals = lax.psum(partial_bias.astype(jnp.bfloat16), "pair").astype(jnp.float32)
    row_offsets = lax.dynamic_index_in_dim(offsets_grid, rep_index, 1, False).reshape(-1)
    fields = jax.vmap(window_fields)(row_offsets, bias_totals)
    force_bias = lax.dynamic_slice_in_dim(bias_totals, pair_index * walk_count, walk_count, 0)
    partial_potential = jnp.einsum(
        "jg,gpq->jpq", fields, cholesky, preferred_element_type=jnp.float32
    )
    summed_potential = lax.psum(partial_potential.astype(jnp.bfloat16), "sub").astype(jnp.float32)
    potential = lax.all_to_all(
        (field_scale * summed_potential).astype(jnp.bfloat16),
        "pair",
        split_axis=0,
        concat_axis=1,
        tiled=True,
    )
    taylor_term = walkers
    summed = walkers.astype(jnp.float32)
    for degree in range(1, TAYLOR + 1):
        product = jnp.einsum(
            "wpq,wqi->wpi", potential, taylor_term, preferred_element_type=jnp.float32
        )
        taylor_term = (product / jnp.float32(degree)).astype(jnp.bfloat16)
        summed = summed + taylor_term.astype(jnp.float32)
    propagated = summed.astype(jnp.bfloat16)
    portion = lax.all_gather(propagated, "pair", axis=0, tiled=True)
    row_count = portion.shape[0]
    positions = jnp.arange(row_count, dtype=jnp.int32)
    selector = (parents[:, None] == positions[None, :]).astype(jnp.bfloat16)
    chosen = jnp.einsum("kr,rpi->kpi", selector, portion, preferred_element_type=jnp.float32)
    new_walkers = chosen.astype(jnp.bfloat16)
    return (new_walkers, force_bias)


def solution(mesh):
    in_specs = (
        P("sub", "pair", None),
        P(),
        P(("grp", "pair", "rep"), None, "sub"),
        P(("grp", "pair", "rep"), None, None),
        P("grp"),
        P("grp"),
        P(("grp", "pair", "rep")),
    )
    out_specs = (P(("grp", "pair", "rep"), None, "sub"), P(("grp", "pair", "rep"), "sub"))
    return jax.shard_map(shards, mesh=mesh, in_specs=in_specs, out_specs=out_specs, check_vma=False)
```

profile of v0, /device:TPU:0, one launch (start us, length us, event | category | flops | bytes accessed | tf_op | source)
XLA Modules:
  0.0 202.1 jit_solution(5442826918399444335)
XLA Ops:
  7.2 0.0 copy-start
  7.2 2.6 %all_gather.6 = bf16[2,640,192]{1,2,0:T(8,128)(2,1)S(1)} all-gather(bf16[2,640,96]{1,2,0:T(8,128)(2,1)} %param.9), channel_id=1, replica_groups=mesh['grp'=2,'pair'=4,'rep'=2,'sub'=2] {'sub'}, dimensions={2}, use_global_device_ids=true | all-gather | bytes 737280 | tf_op jit(solution)/shard_map/all_gather | solution.py:23
  9.8 0.0 copy-start.4
  9.8 0.0 copy-start.1
  9.8 1.3 convolution_convert_fusion
  11.1 1.8 copy.23
  12.9 6.2 %all-to-all-start = ((bf16[2,640,192]{2,0,1:T(2,128)(2,1)}), bf16[2,640,192]{2,0,1:T(2,128)(2,1)S(1)}, u32[]{:S(2)}, u32[]{:S(2)}) async-start(bf16[2,640,192]{2,0,1:T(2,128)(2,1)} %copy.23), calls=%async_computation | async-start | bytes 1310720 | tf_op jit(solution)/shard_map/all_to_all | solution.py:27
  19.1 0.0 all-reduce.2.cloned.1.call-start
  19.1 0.0 copy-done.4
  19.1 0.1 reshape.56
  19.2 0.1 add.78
  19.3 0.1 fusion.35
  19.4 0.0 copy-done.1
  19.4 4.5 %gather_fusion = f32[1024]{0:T(1024)S(1)} fusion(f32[1024]{0:T(1024)S(1)} %copy-done.1, s32[1024]{0:T(1024)S(1)} %fusion.35), kind=kCustom, calls=%fused_computation | custom fusion | bytes 12288 | tf_op jit(solution)/shard_map/vmap()/gather | solution.py:35
  23.9 12.8 %all-to-all-done = bf16[2,640,192]{2,0,1:T(2,128)(2,1)S(1)} async-done(((bf16[2,640,192]{2,0,1:T(2,128)(2,1)}), bf16[2,640,192]{2,0,1:T(2,128)(2,1)S(1)}, u32[]{:S(2)}, u32[]{:S(2)}) %all-to-all-start) | async-done | bytes 491552 | tf_op jit(solution)/shard_map/all_to_all | solution.py:27
  36.7 0.1 copy.24
  36.8 0.7 copy.25
  37.5 0.6 all_to_all.29
  38.1 0.0 copy-done
  38.1 29.4 %fusion.26 = bf16[8,128]{1,0:T(8,128)(2,1)S(1)} fusion(bf16[8,160,192]{2,0,1:T(8,128)(2,1)S(1)} %all_to_all.29, bf16[128,160,640]{2,1,0:T(8,128)(2,1)} %param.7, bf16[640,192]{0,1:T(8,128)(2,1)S(1)} %copy-done), kind=kOutput, calls=%fused_computation.26 | convolution fusion | flops 5100012544 | bytes 26953728 | tf_op jit(solution)/shard_map/jpi,gpi->jg/dot_general | solution.py:28
  67.5 9.8 %psum.14 = bf16[8,128]{1,0:T(8,128)(2,1)S(1)} all-reduce(bf16[8,128]{1,0:T(8,128)(2,1)S(1)} %fusion.26), channel_id=1, replica_groups=mesh['grp'=2,'pair'=4,'rep'=2,'sub'=2] {'pair'}, use_global_device_ids=true, to_apply=%region_0.0 | all-reduce | flops 1024 | bytes 4096 | tf_op jit(solution)/shard_map/psum | solution.py:39
  77.3 26.5 %fusion.10 = bf16[8,160,640]{2,0,1:T(8,128)(2,1)} fusion(bf16[128,160,640]{2,1,0:T(8,128)(2,1)} %param.7, f32[1024]{0:T(1024)S(1)} %gather_fusion, bf16[8,128]{1,0:T(8,128)(2,1)S(1)} %psum.14), kind=kOutput, calls=%fused_computation.8 | convolution fusion | flops 210537472 | bytes 27858944 | tf_op jit(solution)/shard_map/jg,gpq->jpq/dot_general | solution.py:43
  103.8 0.0 all-reduce.2.cloned.1.call-update
  103.8 18.9 %all-reduce.2.cloned.1.call-done = bf16[8,160,640]{2,0,1:T(8,128)(2,1)} async-done(((bf16[8,160,640]{2,0,1:T(8,128)(2,1)}), bf16[8,160,640]{2,0,1:T(8,128)(2,1)}) %all-reduce.2.cloned.1.call-update) | async-done | bytes 1638416 | tf_op jit(solution)/shard_map/psum | solution.py:46
  122.7 1.8 multiply_convert_fusion
  124.4 1.4 copy.28
  125.8 4.9 %all-to-all-start.1 = ((bf16[8,160,640]{2,1,0:T(8,128)(2,1)}), bf16[8,160,640]{2,1,0:T(8,128)(2,1)S(1)}, u32[]{:S(2)}, u32[]{:S(2)}) async-start(bf16[8,160,640]{2,1,0:T(8,128)(2,1)} %copy.28), calls=%async_computation.1 | async-start | bytes 3276800 | tf_op jit(solution)/shard_map/all_to_all | solution.py:47
  130.7 0.6 constant_dynamic-slice_fusion
  131.3 38.2 %all-to-all-done.1 = bf16[8,160,640]{2,1,0:T(8,128)(2,1)S(1)} async-done(((bf16[8,160,640]{2,1,0:T(8,128)(2,1)}), bf16[8,160,640]{2,1,0:T(8,128)(2,1)S(1)}, u32[]{:S(2)}, u32[]{:S(2)}) %all-to-all-start.1) | async-done | bytes 1638432 | tf_op jit(solution)/shard_map/all_to_all | solution.py:47
  169.5 0.0 copy-start.2
  169.5 0.1 copy.29
  169.6 0.8 copy-done.2
  170.4 0.6 convolution_convert_fusion.1
  171.1 0.6 fusion.13
  171.7 0.6 fusion.14
  172.3 0.6 fusion.15
  173.0 0.6 fusion.16
  173.6 0.0 copy-start.3
  173.6 0.7 fusion.20
  174.3 19.8 %all_gather.7 = bf16[8,640,96]{1,2,0:T(8,128)(2,1)S(1)} all-gather(bf16[2,640,96]{1,2,0:T(8,128)(2,1)S(1)} %fusion.20), channel_id=1, replica_groups=mesh['grp'=2,'pair'=4,'rep'=2,'sub'=2] {'pair'}, dimensions={0}, use_global_device_ids=true | all-gather | bytes 1228800 | tf_op jit(solution)/shard_map/all_gather | solution.py:63
  194.0 0.0 copy-done.3
  194.0 0.5 convolution_convert_fusion.2
  194.6 0.7 copy.31
  (2 shorter events, 0.0 us)
Async XLA Ops:
  7.2 30.9 %copy-start = (bf16[640,192]{0,1:T(8,128)(2,1)S(1)}, bf16[640,192]{0,1:T(8,128)(2,1)}, u32[]{:S(2)}) copy-start(bf16[640,192]{0,1:T(8,128)(2,1)} %param.8) | copy-start | bytes 737284
  9.8 9.4 %copy-start.4 = (s32[16]{0:T(128)S(1)}, s32[16]{0:T(128)}, u32[]{:S(2)}) copy-start(s32[16]{0:T(128)} %param.12) | copy-start | bytes 196
  9.8 9.6 %copy-start.1 = (f32[1024]{0:T(1024)S(1)}, f32[1024]{0:T(1024)}, u32[]{:S(2)}) copy-start(f32[1024]{0:T(1024)} %param.11) | copy-start | bytes 12292
  12.9 23.8 %all-to-all-start = ((bf16[2,640,192]{2,0,1:T(2,128)(2,1)}), bf16[2,640,192]{2,0,1:T(2,128)(2,1)S(1)}, u32[]{:S(2)}, u32[]{:S(2)}) async-start(bf16[2,640,192]{2,0,1:T(2,128)(2,1)} %copy.23), calls=%async_computation | async-start | bytes 1310720 | tf_op jit(solution)/shard_map/all_to_all | solution.py:27
  19.1 103.6 %all-reduce.2.cloned.1.call-start = ((), (), s32[]{:S(2)}) async-start(), calls=%async_computation.2 | async-start | bytes 3276800 | tf_op jit(solution)/shard_map/psum | solution.py:46
  125.8 43.7 %all-to-all-start.1 = ((bf16[8,160,640]{2,1,0:T(8,128)(2,1)}), bf16[8,160,640]{2,1,0:T(8,128)(2,1)S(1)}, u32[]{:S(2)}, u32[]{:S(2)}) async-start(bf16[8,160,640]{2,1,0:T(8,128)(2,1)} %copy.28), calls=%async_computation.1 | async-start | bytes 3276800 | tf_op jit(solution)/shard_map/all_to_all | solution.py:47
  169.5 0.9 copy-start.2
  173.6 20.4 %copy-start.3 = (s32[2]{0:T(128)S(1)}, s32[2]{0:T(128)}, u32[]{:S(2)}) copy-start(s32[2]{0:T(128)} %param.13) | copy-start | bytes 28
Sparse Core Ops, SparseCore 0:
  103.9 18.7 all-reduce.1
where the time goes:
time: 202 us
  waiting for transfers between devices  69.9 us (35%)
  matrix products  61.5 us (30%)
  blocking collectives  32.2 us (16%)
  between operations  14.1 us (7%)
  local copies, waits for them, and re-layouts  11.5 us (6%)
  starting transfers between devices  11.1 us (5%)
    all_to_all x1, waiting for transfers between devices, shards(): lax.all_to_all((field_scale * summed_potential).astype(jnp.bfloat16), 'pa...  38.2 us
    dot_general x1, matrix products, shards(): jnp.einsum('jpi,gpi->jg', mixed_rows, half_rotated, preferred_element_typ...  29.4 us
    dot_general x1, matrix products, shards(): jnp.einsum('jg,gpq->jpq', fields, cholesky, preferred_element_type=jnp.fl...  26.5 us
    all_gather x1, blocking collectives, shards(): portion = lax.all_gather(propagated, 'pair', axis=0, tiled=True)  19.8 us
    psum x1, waiting for transfers between devices, shards(): lax.psum(partial_potential.astype(jnp.bfloat16), 'sub').astype(jnp.float32)  18.9 us
    all_to_all x1, waiting for transfers between devices, shards(): lax.all_to_all(mixed, 'pair', split_axis=1, concat_axis=0, tiled=True)  12.8 us
    psum x1, blocking collectives, shards(): lax.psum(partial_bias.astype(jnp.bfloat16), 'pair').astype(jnp.float32)  9.84 us
    all_to_all x1, starting transfers between devices, shards(): lax.all_to_all(mixed, 'pair', split_axis=1, concat_axis=0, tiled=True)  6.24 us
  transfers between devices with their start and end apart: 3, of which 3 were waited for; matrix products, arithmetic and copies ran while one was open for 3% of the time, Pallas kernels for 0%

commit v1 on v0

v1 whole, which is shorter than its diff:
```python
import functools

import jax
import jax.numpy as jnp
from jax import lax
from jax.experimental import pallas as pl
from jax.experimental.pallas import tpu as pltpu
from jax.sharding import PartitionSpec as P

TAYLOR = 6
GROUP = 16
LANES = 128

field_scale = 1.6

MESH = pl.DeviceIdType.MESH
F32 = jnp.float32
BF16 = jnp.bfloat16
NT = (((1,), (1,)), ((), ()))


def step_kernel(
    n, chol, trial, walk, inverse, halves, drawn, picks,
    pot_out, halves_out, bias_out,
    cbuf, mixed, mixbuf, rbuf, ybuf, ebuf, fbsend, fbbuf, fpad, kron, tmp, keep, psend, precv, pfin,
    csem, msem, ssem, hsem, rsem, fsem, qsem, psem, osem,
):
    a = lax.axis_index("pair")
    s = lax.axis_index("sub")
    groups, count = cbuf.shape[0], cbuf.shape[1]
    orbitals = chol.shape[2]
    electrons = walk.shape[2]
    walks = 2 * n
    wide = walks * GROUP
    deep = count * GROUP

    def chol_copy(j):
        return pltpu.make_async_copy(
            chol.at[:, pl.ds(pl.multiple_of(j * GROUP, GROUP), GROUP), :], cbuf.at[j], csem.at[j]
        )

    @pl.loop(0, groups)
    def _(j):
        chol_copy(j).start()

    peers = [(d, lax.rem(a + d, n)) for d in range(1, n)]

    def remote(src, dst, sems, d, target):
        return pltpu.make_async_remote_copy(
            src_ref=src, dst_ref=dst, send_sem=sems.at[0, d], recv_sem=sems.at[1, d],
            device_id=target, device_id_type=MESH,
        )

    barrier = pltpu.get_barrier_semaphore()
    pl.semaphore_signal(barrier, inc=1, device_id={"sub": 1 - s}, device_id_type=MESH)
    for _, b in peers:
        pl.semaphore_signal(barrier, inc=1, device_id={"pair": b}, device_id_type=MESH)

    own_halves = pltpu.make_async_copy(halves, halves_out.at[a], osem.at[0])
    own_halves.start()
    for b in range(n):
        mixed[b] = jnp.dot(walk[b], inverse[...], preferred_element_type=F32).astype(BF16)
    mixbuf[s, a] = mixed[a]
    rbuf[:, a] = picks[...]
    pl.semaphore_wait(barrier, n)

    mixed_copies = [remote(mixed.at[b], mixbuf.at[s, a], msem, d, {"pair": b}) for d, b in peers]
    pick_copies = [remote(picks, rbuf.at[:, a], rsem, d, {"pair": b}) for d, b in peers]
    half_copies = [remote(halves, halves_out.at[a], hsem, d, {"pair": b}) for d, b in peers]
    for copy in mixed_copies + pick_copies:
        copy.start()

    ybuf[...] = jnp.zeros_like(ybuf)
    fpad[...] = jnp.zeros_like(fpad)
    ebuf[...] = jnp.where(
        lax.broadcasted_iota(jnp.int32, (count, deep), 1) // GROUP
        == lax.broadcasted_iota(jnp.int32, (count, deep), 0), 1.0, 0.0
    ).astype(BF16)

    for copy in mixed_copies:
        copy.wait_recv()
    across = remote(mixbuf.at[s], mixbuf.at[s], ssem, 0, {"sub": 1 - s})
    across.start()
    for copy in half_copies:
        copy.start()
    across.wait_recv()

    tile = max(GROUP, min(deep, 65536 // wide) // GROUP * GROUP)

    @pl.loop(0, groups)
    def _(j):
        chol_copy(j).wait()
        rows = mixbuf[:, :, pl.ds(pl.multiple_of(j * GROUP, GROUP), GROUP), :]
        density = lax.dot_general(
            rows.reshape(wide, electrons), trial[...], NT, preferred_element_type=F32
        ).astype(BF16)
        part = tile // GROUP

        @pl.loop(0, deep // tile)
        def _(t):
            block = cbuf[j, pl.ds(t * part, part)].reshape(tile, orbitals)
            at = pl.ds(pl.multiple_of(t * tile, tile), tile)
            ybuf[at, :] += lax.dot_general(block, density, NT, preferred_element_type=F32)

    same = (
        lax.broadcasted_iota(jnp.int32, (1, GROUP, wide), 1)
        == lax.broadcasted_iota(jnp.int32, (1, GROUP, wide), 2) % GROUP
    )
    traced = jnp.sum(jnp.where(same, ybuf[...].reshape(count, GROUP, wide), 0.0), axis=1)
    adder = jnp.where(
        lax.broadcasted_iota(jnp.int32, (walks, wide), 1) // GROUP
        == lax.broadcasted_iota(jnp.int32, (walks, wide), 0), 1.0, 0.0
    )
    partial = lax.dot_general(
        adder, traced, NT, preferred_element_type=F32, precision=lax.Precision.HIGHEST
    )
    fbsend[...] = partial
    fbbuf[a] = partial
    bias_copies = [remote(fbsend, fbbuf.at[a], fsem, d, {"pair": b}) for d, b in peers]
    for copy in bias_copies:
        copy.start()
    for copy in bias_copies + pick_copies:
        copy.wait_recv()
    total = jnp.sum(fbbuf[...], axis=0)
    bias_out[...] = total
    fpad[0:walks, :] = drawn[...] - total
    fields = fpad[...].astype(BF16)

    step = 8 * GROUP
    chunks = wide // step

    @pl.loop(0, chunks)
    def _(c):
        chosen = rbuf[...].reshape(chunks, step, LANES) if chunks == 1 else None
        if chunks == 1:
            chosen = chosen[0]
        else:
            per = n // 8
            chosen = rbuf[c // per, pl.ds(lax.rem(c, per) * 8, 8)].reshape(step, LANES)
        spread = jnp.dot(chosen, fields, preferred_element_type=F32).astype(BF16)
        full = jnp.dot(spread, ebuf[...], preferred_element_type=F32)
        diagonal = (
            lax.broadcasted_iota(jnp.int32, (step, deep), 0) % GROUP
            == lax.broadcasted_iota(jnp.int32, (step, deep), 1) % GROUP
        )
        kron[c] = jnp.where(diagonal, full, 0.0).astype(BF16)

    def part_copy(j):
        return pltpu.make_async_remote_copy(
            src_ref=psend.at[j], dst_ref=precv.at[j], send_sem=qsem.at[0, j], recv_sem=qsem.at[1, j],
            device_id={"sub": 1 - s}, device_id_type=MESH,
        )

    def pot_copy(d, b, j):
        at = pl.ds(pl.multiple_of(j * GROUP, GROUP), GROUP)
        return pltpu.make_async_remote_copy(
            src_ref=pfin.at[b, at], dst_ref=pot_out.at[a, at],
            send_sem=psem.at[0, d, j], recv_sem=psem.at[1, d, j],
            device_id={"pair": b}, device_id_type=MESH,
        )

    def finish(j):
        part_copy(j).wait_recv()
        at = pl.ds(pl.multiple_of(j * GROUP, GROUP), GROUP)
        pfin[:, at, :] = (field_scale * (keep[j] + precv[j].astype(F32))).astype(BF16)
        for d, b in peers:
            pot_copy(d, b, j).start()

    @pl.loop(0, groups)
    def _(j):
        @pl.loop(0, chunks)
        def _(c):
            tmp[pl.ds(c * 8, 8)] = jnp.dot(
                kron[c], cbuf[j].reshape(deep, orbitals), preferred_element_type=F32
            ).reshape(8, GROUP, orbitals)

        psend[j] = tmp[pl.ds((1 - s) * n, n)].astype(BF16)
        part_copy(j).start()
        keep[j] = tmp[pl.ds(s * n, n)]

        @pl.when(j > 0)
        def _():
            finish(j - 1)

    finish(groups - 1)
    own_pot = pltpu.make_async_copy(pfin.at[a], pot_out.at[a], osem.at[1])
    own_pot.start()
    across.wait_send()
    for copy in mixed_copies + pick_copies + bias_copies:
        copy.wait_send()
    for copy in half_copies:
        copy.wait()
    own_halves.wait()

    @pl.loop(0, groups)
    def _(j):
        part_copy(j).wait_send()
        for d, b in peers:
            pot_copy(d, b, j).wait()

    own_pot.wait()


def shards(cholesky, trial_orbitals, walkers, intersection_inverse, noise_stream, offsets, parents):
    count, rows, orbitals = cholesky.shape
    walk_count, _, half = walkers.shape
    electrons = trial_orbitals.shape[1]
    n = lax.axis_size("pair")
    rep_size = lax.axis_size("rep")
    pair_index = lax.axis_index("pair")
    rep_index = lax.axis_index("rep")
    sub_index = lax.axis_index("sub")
    assert walk_count == 2 and lax.axis_size("sub") == 2
    padded = -(-rows // GROUP) * GROUP
    groups = padded // GROUP
    walks = walk_count * n
    wide, deep = walks * GROUP, count * GROUP
    if padded != rows:
        cholesky = jnp.pad(cholesky, ((0, 0), (0, padded - rows), (0, 0)))

    whole = lax.all_to_all(walkers, "sub", split_axis=0, concat_axis=2, tiled=True)
    blocks = whole.reshape(n, rows, electrons)
    if padded != rows:
        blocks = jnp.pad(blocks, ((0, 0), (0, padded - rows), (0, 0)))
    inverse = lax.dynamic_index_in_dim(intersection_inverse, sub_index, 0, False)

    offsets_grid = offsets.reshape(n, rep_size, walk_count)
    row_offsets = lax.dynamic_index_in_dim(offsets_grid, rep_index, 1, False).T.reshape(-1)
    wanted = row_offsets[:, None] + sub_index * count + jnp.arange(count, dtype=jnp.int32)[None, :]
    places = jnp.arange(noise_stream.shape[0], dtype=jnp.int32)
    drawn = jnp.sum(
        jnp.where(wanted[:, :, None] == places[None, None, :], noise_stream[None, None, :], 0.0), axis=2
    )

    columns = (parents % walk_count) * n + parents // walk_count
    picks = (columns[:, None] == jnp.arange(LANES, dtype=jnp.int32)[None, :]).astype(BF16)
    picks = jnp.broadcast_to(picks[:, None, :], (walk_count, GROUP, LANES))

    vmem = pl.BlockSpec(memory_space=pltpu.VMEM)
    hbm = pl.BlockSpec(memory_space=pl.ANY)
    dma = pltpu.SemaphoreType.DMA
    potential, gathered, bias = pl.pallas_call(
        functools.partial(step_kernel, n),
        out_shape=(
            jax.ShapeDtypeStruct((n, padded, orbitals), BF16),
            jax.ShapeDtypeStruct((n, walk_count, orbitals, half), BF16),
            jax.ShapeDtypeStruct((walks, count), F32),
        ),
        in_specs=[hbm, vmem, vmem, vmem, vmem, vmem, vmem],
        out_specs=(hbm, hbm, vmem),
        scratch_shapes=[
            pltpu.VMEM((groups, count, GROUP, orbitals), BF16),
            pltpu.VMEM((n, padded, electrons), BF16),
            pltpu.VMEM((2, n, padded, electrons), BF16),
            pltpu.VMEM((2, n, GROUP, LANES), BF16),
            pltpu.VMEM((deep, wide), F32),
            pltpu.VMEM((count, deep), BF16),
            pltpu.VMEM((walks, count), F32),
            pltpu.VMEM((n, walks, count), F32),
            pltpu.VMEM((LANES, count), F32),
            pltpu.VMEM((wide // (8 * GROUP), 8 * GROUP, deep), BF16),
            pltpu.VMEM((walks, GROUP, orbitals), F32),
            pltpu.VMEM((groups, n, GROUP, orbitals), F32),
            pltpu.VMEM((groups, n, GROUP, orbitals), BF16),
            pltpu.VMEM((groups, n, GROUP, orbitals), BF16),
            pltpu.VMEM((n, padded, orbitals), BF16),
            dma((groups,)),
            dma((2, n)),
            dma((2, 1)),
            dma((2, n)),
            dma((2, n)),
            dma((2, n)),
            dma((2, groups)),
            dma((2, n, groups)),
            dma((2,)),
        ],
        compiler_params=pltpu.CompilerParams(
            collective_id=0, has_side_effects=True, vmem_limit_bytes=52 * 1024 * 1024
        ),
    )(cholesky, trial_orbitals, blocks, inverse, walkers, drawn, picks)

    potential = potential[:, :rows].reshape(orbitals, orbitals)
    selector = picks[:, 0, :walks].reshape(walk_count, walk_count, n)
    chosen = jnp.einsum("ckb,bkpi->cpi", selector, gathered, preferred_element_type=F32).astype(BF16)
    taylor_term = lax.all_to_all(chosen, "sub", split_axis=0, concat_axis=2, tiled=True)[0]
    summed = taylor_term.astype(F32)
    for degree in range(1, TAYLOR + 1):
        product = jnp.dot(potential, taylor_term, preferred_element_type=F32)
        taylor_term = (product / jnp.float32(degree)).astype(BF16)
        summed = summed + taylor_term.astype(F32)
    propagated = summed.astype(BF16)
    new_walkers = lax.all_to_all(propagated[None], "sub", split_axis=2, concat_axis=0, tiled=True)
    by_walker = bias.reshape(walk_count, n, count)
    force_bias = lax.dynamic_index_in_dim(by_walker, pair_index, 1, False)
    return (new_walkers, force_bias)


def solution(mesh):
    in_specs = (
        P("sub", "pair", None),
        P(),
        P(("grp", "pair", "rep"), None, "sub"),
        P(("grp", "pair", "rep"), None, None),
        P("grp"),
        P("grp"),
        P(("grp", "pair", "rep")),
    )
    out_specs = (P(("grp", "pair", "rep"), None, "sub"), P(("grp", "pair", "rep"), "sub"))
    return jax.shard_map(shards, mesh=mesh, in_specs=in_specs, out_specs=out_specs, check_vma=False)
```

time: 202 us -> 97.2 us (0.48)
  waiting for transfers between devices: 69.9 us -> 0.01 us
  Pallas kernels: 0 us -> 67.4 us
  matrix products: 61.5 us -> 3.54 us
  blocking collectives: 32.2 us -> 7.84 us
  between operations: 14.1 us -> 0.81 us
  starting transfers between devices: 11.1 us -> 3.58 us
  other arithmetic: 1.86 us -> 4.32 us
  local copies, waits for them, and re-layouts: 11.5 us -> 9.33 us
    pallas_call x0 -> x1, Pallas kernels: none -> 67.4 us  [shards(): pl.pallas_call(functools.partial(step_kernel, n), out_shape=(jax.ShapeDty...]
    dot_general x10 -> x7, matrix products: 61.5 us -> 3.54 us  [the longest x6 2.63 us: shards(): product = jnp.dot(potential, taylor_term, preferred_element_type=F32)]
    all_to_all x2 -> x1, waiting for transfers between devices: 51 us -> 0.01 us  [shards(): lax.all_to_all(walkers, 'sub', split_axis=0, concat_axis=2, tiled=True)]
    all_gather x2 -> x0, blocking collectives: 22.3 us -> none  [the longest x1 19.8 us: shards(): portion = lax.all_gather(propagated, 'pair', axis=0, tiled=True)]
    psum x1 -> x0, waiting for transfers between devices: 18.9 us -> none  [shards(): lax.psum(partial_potential.astype(jnp.bfloat16), 'sub').astype(jnp.float32)]
    psum x1 -> x0, blocking collectives: 9.84 us -> none  [shards(): lax.psum(partial_bias.astype(jnp.bfloat16), 'pair').astype(jnp.float32)]
    all_to_all x0 -> x2, blocking collectives: none -> 7.84 us  [the longest x1 3.92 us: shards(): lax.all_to_all(chosen, 'sub', split_axis=0, concat_axis=2, tiled=True)[0]]
    all_to_all x2 -> x1, starting transfers between devices: 11.1 us -> 3.58 us  [shards(): lax.all_to_all(walkers, 'sub', split_axis=0, concat_axis=2, tiled=True)]
  transfers between devices with their start and end apart: 3 -> 1, of which waited for: 3 -> 0; matrix products, arithmetic and copies ran while one was open for 3% -> 3% of each run, Pallas kernels for 0% -> 0%
where the time goes in v1:
time: 97.2 us; the launch traced here: 96.8 us
  Pallas kernels  67.4 us (69%)
  local copies, waits for them, and re-layouts  9.33 us (10%)
  blocking collectives  7.84 us (8%)
  other arithmetic  4.32 us (4%)
  starting transfers between devices  3.58 us (4%)
  matrix products  3.54 us (4%)
    pallas_call x1, Pallas kernels, shards(): pl.pallas_call(functools.partial(step_kernel, n), out_shape=(jax.ShapeDty...  67.4 us
    unnamed x9, local copies, waits for them, and re-layouts  3.96 us
    all_to_all x1, blocking collectives, shards(): lax.all_to_all(chosen, 'sub', split_axis=0, concat_axis=2, tiled=True)[0]  3.92 us
    all_to_all x1, blocking collectives, shards(): lax.all_to_all(propagated[None], 'sub', split_axis=2, concat_axis=0, tile...  3.92 us
    all_to_all x1, starting transfers between devices, shards(): lax.all_to_all(walkers, 'sub', split_axis=0, concat_axis=2, tiled=True)  3.58 us
    pallas_call x1, local copies, waits for them, and re-layouts, shards(): pl.pallas_call(functools.partial(step_kernel, n), out_shape=(jax.ShapeDty...  2.89 us
    dot_general x6, matrix products, shards(): product = jnp.dot(potential, taylor_term, preferred_element_type=F32)  2.63 us
    unnamed x1, other arithmetic  2.16 us
  transfers between devices with their start and end apart: 1, of which 0 were waited for; matrix products, arithmetic and copies ran while one was open for 3% of the time, Pallas kernels for 0%

profile of v1, /device:TPU:0, one launch (start us, length us, event | category | flops | bytes accessed | tf_op | source)
XLA Modules:
  0.0 96.8 jit_solution(10600510488885091578)
XLA Ops:
  0.6 0.0 copy-start
  0.6 3.6 %all-to-all-start = ((bf16[2,640,96]{1,2,0:T(8,128)(2,1)}), bf16[2,640,96]{1,2,0:T(8,128)(2,1)S(1)}, u32[]{:S(2)}, u32[]{:S(2)}) async-start(bf16[2,640,96]{1,2,0:T(8,128)(2,1)} %param.9), calls=%async_computation | async-start | bytes 491520 | tf_op jit(solution)/shard_map/all_to_all | solution.py:221
  4.2 1.2 %copy.49.halves = bf16[2,640,96]{2,1,0:T(8,128)(2,1)S(1)} copy(bf16[2,640,96]{1,2,0:T(8,128)(2,1)} %param.9) | data formatting | bytes 491520 | tf_op args[2]
  5.4 0.7 reshape.70
  6.2 0.1 copy.56
  6.3 0.1 add.85
  6.4 0.1 iota_add_fusion
  6.5 0.7 fusion.13
  7.1 0.1 iota_compare_fusion.1
  7.2 0.0 all-to-all-done
  7.2 0.3 reshape.69
  7.5 0.3 copy.48.walk
  7.8 1.1 %copy.47.trial = bf16[640,192]{1,0:T(8,128)(2,1)S(1)} copy(bf16[640,192]{0,1:T(8,128)(2,1)} %param.8) | data formatting | bytes 491520 | tf_op args[1]
  8.9 1.3 %select_reduce_fusion.drawn = f32[8,128]{1,0:T(8,128)S(1)} fusion(f32[1024]{0:T(1024)} %param.11, s32[8,128]{1,0:T(8,128)S(1)} %iota_add_fusion), kind=kLoop, calls=%fused_computation | loop fusion | flops 3144704 | bytes 12288 | tf_op jit(solution)/shard_map/reduce_sum | solution.py:231
  10.2 0.0 copy-done
  10.3 67.4 %shard_map.86 = (bf16[4,160,640]{2,1,0:T(8,128)(2,1)S(1)}, bf16[4,2,640,96]{3,2,1,0:T(8,128)(2,1)}, f32[8,128]{1,0:T(8,128)S(1)}) custom-call(bf16[128,160,640]{2,1,0:T(8,128)(2,1)} %chol.1, bf16[640,192]{1,0:T(8,128)(2,1)S(1)} %copy.47.trial, bf16[4,160,192]{2,1,0:T(8,128)(2,1)S(1)} %copy.48.walk, bf16[192,192]{1,0:T(8,128)(2,1)S(1)} %dynamic-slice_bitcast_fusion.inverse, ...), custom_call_target="tpu_custom_call" | custom-call | tf_op jit(solution)/shard_map/pallas_call | solution.py:242
  77.7 2.9 %copy.51 = bf16[4,2,640,96]{2,0,1,3:T(4,128)(2,1)S(1)} copy(bf16[4,2,640,96]{3,2,1,0:T(8,128)(2,1)} %get-tuple-element.5) | data formatting | bytes 1966080 | tf_op jit(solution)/shard_map/pallas_call | solution.py:242
  80.5 0.1 broadcast_in_dim.18.clone
  80.6 0.9 fusion
  81.6 3.9 %all_to_all.48 = bf16[2,640,96]{1,2,0:T(8,128)(2,1)S(1)} all-to-all(bf16[2,640,96]{1,2,0:T(8,128)(2,1)S(1)} %copy.52), channel_id=1, replica_groups=mesh['grp'=2,'pair'=4,'rep'=2,'sub'=2] {'sub'}, dimensions={0} | all-to-all | bytes 491520 | tf_op jit(solution)/shard_map/all_to_all | solution.py:285
  85.5 0.4 convolution_convert_fusion
  85.9 0.4 fusion.1
  86.4 0.4 fusion.2
  86.8 0.4 fusion.3
  87.3 0.4 fusion.4
  87.7 0.5 fusion.9
  88.2 0.4 copy.62
  88.6 0.5 broadcast.62
  89.1 2.2 %reduce = bf16[192,640]{1,0:T(8,128)(2,1)S(1)} reduce(bf16[192,1,640]{2,1,0:T(2,128)(2,1)S(1)} %bitcast.61, bf16[]{:T(256)} %broadcast.62), dimensions={1}, to_apply=%bitcast.52.reduce_sub_computation | reduce | bytes 491522
  91.2 0.1 reshape.75
  91.3 3.9 %all_to_all.49 = bf16[2,2,30720]{2,1,0:T(2,128)(2,1)S(1)} all-to-all(bf16[2,2,30720]{2,1,0:T(2,128)(2,1)S(1)} %reshape.75), channel_id=1, replica_groups=mesh['grp'=2,'pair'=4,'rep'=2,'sub'=2] {'sub'}, dimensions={0} | all-to-all | bytes 491520 | tf_op jit(solution)/shard_map/all_to_all | solution.py:292
  95.2 0.2 reshape.76
  95.5 0.7 copy.55
  96.2 0.6 constant_dynamic-slice_fusion
  (5 shorter events, 0.1 us)
Async XLA Ops:
  0.6 9.6 %copy-start = (bf16[2,192,192]{2,1,0:T(8,128)(2,1)S(1)}, bf16[2,192,192]{2,1,0:T(8,128)(2,1)}, u32[]{:S(2)}) copy-start(bf16[2,192,192]{2,1,0:T(8,128)(2,1)} %param.10) | copy-start | bytes 442372
  0.6 6.6 %all-to-all-start = ((bf16[2,640,96]{1,2,0:T(8,128)(2,1)}), bf16[2,640,96]{1,2,0:T(8,128)(2,1)S(1)}, u32[]{:S(2)}, u32[]{:S(2)}) async-start(bf16[2,640,96]{1,2,0:T(8,128)(2,1)} %param.9), calls=%async_computation | async-start | bytes 491520 | tf_op jit(solution)/shard_map/all_to_all | solution.py:221

commit v2 on v1

v2 whole, which is shorter than its diff:
```python
import functools

import jax
import jax.numpy as jnp
from jax import lax
from jax.experimental import pallas as pl
from jax.experimental.pallas import tpu as pltpu
from jax.sharding import PartitionSpec as P

TAYLOR = 6
GROUP = 16
LANES = 128

field_scale = 1.6

MESH = pl.DeviceIdType.MESH
F32 = jnp.float32
BF16 = jnp.bfloat16
NT = (((1,), (1,)), ((), ()))


def step_kernel(
    n, rows, chol, trial, inverse, walkers, drawn, picks, parents,
    walkers_out, bias_out,
    cbuf, wfirst, mixed, mixbuf, wbuf, rbuf, ybuf, ebuf, fbsend, fbbuf, fpad, kron, tmp, keep, psend, precv,
    pfin, pot, xbuf, xsend, done, obuf,
    csem, ssem, msem, xsem, hsem, rsem, fsem, qsem, psem,
):
    a = lax.axis_index("pair")
    s = lax.axis_index("sub")
    groups, count = cbuf.shape[0], cbuf.shape[1]
    electrons, orbitals = trial.shape
    padded = groups * GROUP
    walks = 2 * n
    wide = walks * GROUP
    deep = count * GROUP

    def chol_copy(j):
        return pltpu.make_async_copy(
            chol.at[:, pl.ds(pl.multiple_of(j * GROUP, GROUP), GROUP), :], cbuf.at[j], csem.at[j]
        )

    @pl.loop(0, groups)
    def _(j):
        chol_copy(j).start()

    peers = [(d, lax.rem(a + d, n)) for d in range(1, n)]
    sibling = {"sub": 1 - s}

    def remote(src, dst, sems, place, target):
        return pltpu.make_async_remote_copy(
            src_ref=src, dst_ref=dst, send_sem=sems.at[(0,) + place], recv_sem=sems.at[(1,) + place],
            device_id=target, device_id_type=MESH,
        )

    barrier = pltpu.get_barrier_semaphore()
    pl.semaphore_signal(barrier, inc=1, device_id=sibling, device_id_type=MESH)
    for _, b in peers:
        pl.semaphore_signal(barrier, inc=1, device_id={"pair": b}, device_id_type=MESH)
    pl.semaphore_wait(barrier, n)

    first_copy = remote(walkers.at[1 - s], wfirst.at[s], ssem, (0,), sibling)
    first_copy.start()
    pick_copies = [remote(picks, rbuf.at[:, a], rsem, (d,), {"pair": b}) for d, b in peers]
    for copy in pick_copies:
        copy.start()
    wfirst[s] = walkers[s]
    wbuf[pl.ds(2 * a, 2)] = walkers[...]
    rbuf[:, a] = picks[...]
    if padded != rows:
        spot = lax.broadcasted_iota(jnp.int32, (orbitals, n * padded), 1)
        spot = jnp.where(spot % padded < rows, spot // padded * rows + spot % padded, -1)
        layout = jnp.where(
            spot == lax.broadcasted_iota(jnp.int32, (orbitals, n * padded), 0), 1.0, 0.0
        ).astype(BF16)
    first_copy.wait_recv()
    start = wfirst[...].reshape(electrons, orbitals)
    if padded != rows:
        start = jnp.dot(start, layout, preferred_element_type=F32).astype(BF16)
    mixed[...] = lax.dot_general(
        start, inverse[s], (((0,), (0,)), ((), ())), preferred_element_type=F32
    ).astype(BF16).reshape(n, padded, electrons)

    split = max(1, groups // 2)
    parts = [pl.ds(0, split * GROUP), pl.ds(split * GROUP, (groups - split) * GROUP)]
    mixed_copies = [
        [remote(mixed.at[b, part], mixbuf.at[s, a, part], msem, (h, d), {"pair": b}) for d, b in peers]
        for h, part in enumerate(parts)
    ]
    across_copies = [
        [
            remote(mixbuf.at[s, b, part], mixbuf.at[s, b, part], xsem, (h, d), sibling)
            for d, b in [(d, lax.rem(a + n - d, n)) for d in range(n)]
        ]
        for h, part in enumerate(parts)
    ]
    for h in range(2):
        for copy in mixed_copies[h]:
            copy.start()
    mixbuf[s, a] = mixed[a]

    ybuf[...] = jnp.zeros_like(ybuf)
    fpad[...] = jnp.zeros_like(fpad)
    ebuf[...] = jnp.where(
        lax.broadcasted_iota(jnp.int32, (count, deep), 1) // GROUP
        == lax.broadcasted_iota(jnp.int32, (count, deep), 0), 1.0, 0.0
    ).astype(BF16)

    def chain_copy(way, t):
        block = a - t if way == 0 else a + t
        at = pl.ds(2 * block, 2)
        return remote(wbuf.at[at], wbuf.at[at], hsem, (way, t), {"pair": a + 1 - 2 * way})

    def chain_sends(way, t):
        return (a >= t) & (a + 1 < n) if way == 0 else (a + t < n) & (a > 0)

    def chain_gets(way, t):
        return a >= t + 1 if way == 0 else a + t + 1 < n

    def chain_step(t):
        for way in range(2):
            if t > 0:
                @pl.when(chain_gets(way, t - 1))
                def _():
                    back = a - t if way == 0 else a + t
                    at = pl.ds(2 * back, 2)
                    remote(
                        wbuf.at[at], wbuf.at[at], hsem, (way, t - 1), {"pair": a - 1 + 2 * way}
                    ).wait_recv()
            if t < n - 1:
                @pl.when(chain_sends(way, t))
                def _():
                    chain_copy(way, t).start()

    def pass_across(h):
        across_copies[h][0].start()
        for copy, forward in zip(mixed_copies[h], across_copies[h][1:]):
            copy.wait_recv()
            forward.start()

    tile = max(GROUP, min(deep, 65536 // wide) // GROUP * GROUP)
    share = tile // GROUP

    def bias_group(j):
        chol_copy(j).wait()
        block_rows = mixbuf[:, :, pl.ds(pl.multiple_of(j * GROUP, GROUP), GROUP), :]
        density = jnp.dot(
            block_rows.reshape(wide, electrons), trial[...], preferred_element_type=F32
        ).astype(BF16)

        @pl.loop(0, deep // tile)
        def _(t):
            block = cbuf[j, pl.ds(t * share, share)].reshape(tile, orbitals)
            at = pl.ds(pl.multiple_of(t * tile, tile), tile)
            ybuf[at, :] += lax.dot_general(block, density, NT, preferred_element_type=F32)

    pass_across(0)
    for copy in across_copies[0]:
        copy.wait_recv()
    chain_step(0)
    pl.loop(0, split - 1)(bias_group)
    pass_across(1)
    pl.loop(split - 1, split)(bias_group)
    for copy in across_copies[1]:
        copy.wait_recv()
    late = max(split, groups - 2)
    pl.loop(split, late)(bias_group)
    chain_step(1)
    pl.loop(late, groups)(bias_group)

    same = (
        lax.broadcasted_iota(jnp.int32, (1, GROUP, wide), 1)
        == lax.broadcasted_iota(jnp.int32, (1, GROUP, wide), 2) % GROUP
    )
    traced = jnp.sum(jnp.where(same, ybuf[...].reshape(count, GROUP, wide), 0.0), axis=1)
    adder = jnp.where(
        lax.broadcasted_iota(jnp.int32, (walks, wide), 1) // GROUP
        == lax.broadcasted_iota(jnp.int32, (walks, wide), 0), 1.0, 0.0
    )
    partial = lax.dot_general(
        adder, traced, NT, preferred_element_type=F32, precision=lax.Precision.HIGHEST
    )
    fbsend[...] = partial
    fbbuf[a] = partial
    bias_copies = [remote(fbsend, fbbuf.at[a], fsem, (d,), {"pair": b}) for d, b in peers]
    for copy in bias_copies:
        copy.start()
    for copy in pick_copies + bias_copies:
        copy.wait_recv()
    total = jnp.sum(fbbuf[...], axis=0)
    fpad[0:walks, :] = drawn[...] - total
    fields = fpad[...].astype(BF16)

    step = 8 * GROUP
    chunks = wide // step

    @pl.loop(0, chunks)
    def _(c):
        if chunks == 1:
            chosen = rbuf[...].reshape(step, LANES)
        else:
            per = n // 8
            chosen = rbuf[c // per, pl.ds(lax.rem(c, per) * 8, 8)].reshape(step, LANES)
        spread = jnp.dot(chosen, fields, preferred_element_type=F32).astype(BF16)
        full = jnp.dot(spread, ebuf[...], preferred_element_type=F32)
        diagonal = (
            lax.broadcasted_iota(jnp.int32, (step, deep), 0) % GROUP
            == lax.broadcasted_iota(jnp.int32, (step, deep), 1) % GROUP
        )
        kron[c] = jnp.where(diagonal, full, 0.0).astype(BF16)

    def part_copy(j):
        return remote(psend.at[j], precv.at[j], qsem, (j,), sibling)

    def pot_copy(d, b, j):
        at = pl.ds(pl.multiple_of(j * GROUP, GROUP), GROUP)
        return remote(pfin.at[b, at], pot.at[a, at], psem, (d, j), {"pair": b})

    def finish(j):
        part_copy(j).wait_recv()
        at = pl.ds(pl.multiple_of(j * GROUP, GROUP), GROUP)
        pfin[:, at, :] = (field_scale * (keep[j] + precv[j].astype(F32))).astype(BF16)
        for d, b in peers:
            pot_copy(d, b, j).start()

    def potential_group(j):
        @pl.loop(0, chunks)
        def _(c):
            tmp[pl.ds(c * 8, 8)] = jnp.dot(
                kron[c], cbuf[j].reshape(deep, orbitals), preferred_element_type=F32
            ).reshape(8, GROUP, orbitals)

        psend[j] = tmp[pl.ds((1 - s) * n, n)].astype(BF16)
        part_copy(j).start()
        keep[j] = tmp[pl.ds(s * n, n)]

        @pl.when(j > 0)
        def _():
            finish(j - 1)

    early = min(3, groups)
    pl.loop(0, early)(potential_group)
    if n > 2:
        chain_step(2)
    pl.loop(early, groups)(potential_group)
    finish(groups - 1)
    pot[a] = pfin[a]

    fbsend_rows = fpad.at[0:walks]
    fbsend_rows[...] = total
    for k in range(2):
        bias_out[k : k + 1, :] = fpad[pl.ds(k * n + a, 1), :]

    for t in range(3, n):
        chain_step(t)
    xbuf[s] = wbuf[parents[s]]
    xsend[...] = wbuf[parents[1 - s]]
    child_copy = remote(xsend, xbuf.at[s], ssem, (1,), sibling)
    child_copy.start()
    child_copy.wait_recv()
    term = xbuf[...].reshape(electrons, orbitals)
    summed = term.astype(F32)

    @pl.loop(0, groups)
    def _(j):
        for d, b in peers:
            pot_copy(d, b, j).wait_recv()

    for degree in range(1, TAYLOR + 1):
        product = lax.dot_general(
            term, pot[...].reshape(n * padded, orbitals), NT, preferred_element_type=F32
        )
        term = (product / jnp.float32(degree)).astype(BF16)
        if padded != rows:
            term = lax.dot_general(term, layout, NT, preferred_element_type=F32).astype(BF16)
        summed = summed + term.astype(F32)
    done[...] = summed.astype(BF16).reshape(done.shape)
    last_copy = remote(done.at[1 - s], obuf.at[s], ssem, (2,), sibling)
    last_copy.start()
    obuf[s] = done[s]

    first_copy.wait_send()
    child_copy.wait_send()
    for copy in mixed_copies[0] + mixed_copies[1] + across_copies[0] + across_copies[1]:
        copy.wait_send()
    for copy in pick_copies + bias_copies:
        copy.wait_send()
    for t in range(n - 1):
        for way in range(2):
            @pl.when(chain_sends(way, t))
            def _():
                chain_copy(way, t).wait_send()

    @pl.loop(0, groups)
    def _(j):
        part_copy(j).wait_send()
        for d, b in peers:
            pot_copy(d, b, j).wait_send()

    last_copy.wait()
    walkers_out[...] = obuf[...]


def shards(cholesky, trial_orbitals, walkers, intersection_inverse, noise_stream, offsets, parents):
    count, rows, orbitals = cholesky.shape
    walk_count, _, half = walkers.shape
    electrons = trial_orbitals.shape[1]
    n = lax.axis_size("pair")
    rep_size = lax.axis_size("rep")
    rep_index = lax.axis_index("rep")
    sub_index = lax.axis_index("sub")
    assert walk_count == 2 and lax.axis_size("sub") == 2
    padded = -(-rows // GROUP) * GROUP
    groups = padded // GROUP
    walks = walk_count * n
    wide, deep = walks * GROUP, count * GROUP
    split = max(1, groups // 2)
    if padded != rows:
        cholesky = jnp.pad(cholesky, ((0, 0), (0, padded - rows), (0, 0)))

    offsets_grid = offsets.reshape(n, rep_size, walk_count)
    row_offsets = lax.dynamic_index_in_dim(offsets_grid, rep_index, 1, False).T.reshape(-1)
    wanted = row_offsets[:, None] + sub_index * count + jnp.arange(count, dtype=jnp.int32)[None, :]
    places = jnp.arange(noise_stream.shape[0], dtype=jnp.int32)
    drawn = jnp.sum(
        jnp.where(wanted[:, :, None] == places[None, None, :], noise_stream[None, None, :], 0.0), axis=2
    )

    columns = (parents % walk_count) * n + parents // walk_count
    picks = (columns[:, None] == jnp.arange(LANES, dtype=jnp.int32)[None, :]).astype(BF16)
    picks = jnp.broadcast_to(picks[:, None, :], (walk_count, GROUP, LANES))

    vmem = pl.BlockSpec(memory_space=pltpu.VMEM)
    smem = pl.BlockSpec(memory_space=pltpu.SMEM)
    hbm = pl.BlockSpec(memory_space=pl.ANY)
    dma = pltpu.SemaphoreType.DMA
    new_walkers, force_bias = pl.pallas_call(
        functools.partial(step_kernel, n, rows),
        out_shape=(
            jax.ShapeDtypeStruct((walk_count, half, orbitals), BF16),
            jax.ShapeDtypeStruct((walk_count, count), F32),
        ),
        in_specs=[hbm, vmem, vmem, vmem, vmem, vmem, smem],
        out_specs=(vmem, vmem),
        scratch_shapes=[
            pltpu.VMEM((groups, count, GROUP, orbitals), BF16),
            pltpu.VMEM((2, half, orbitals), BF16),
            pltpu.VMEM((n, padded, electrons), BF16),
            pltpu.VMEM((2, n, padded, electrons), BF16),
            pltpu.VMEM((walks, half, orbitals), BF16),
            pltpu.VMEM((2, n, GROUP, LANES), BF16),
            pltpu.VMEM((deep, wide), F32),
            pltpu.VMEM((count, deep), BF16),
            pltpu.VMEM((walks, count), F32),
            pltpu.VMEM((n, walks, count), F32),
            pltpu.VMEM((LANES, count), F32),
            pltpu.VMEM((wide // (8 * GROUP), 8 * GROUP, deep), BF16),
            pltpu.VMEM((walks, GROUP, orbitals), F32),
            pltpu.VMEM((groups, n, GROUP, orbitals), F32),
            pltpu.VMEM((groups, n, GROUP, orbitals), BF16),
            pltpu.VMEM((groups, n, GROUP, orbitals), BF16),
            pltpu.VMEM((n, padded, orbitals), BF16),
            pltpu.VMEM((n, padded, orbitals), BF16),
            pltpu.VMEM((2, half, orbitals), BF16),
            pltpu.VMEM((half, orbitals), BF16),
            pltpu.VMEM((2, half, orbitals), BF16),
            pltpu.VMEM((2, half, orbitals), BF16),
            dma((groups,)),
            dma((2, 3)),
            dma((2, 2, n)),
            dma((2, 2, n)),
            dma((2, 2, n)),
            dma((2, n)),
            dma((2, n)),
            dma((2, groups)),
            dma((2, n, groups)),
        ],
        compiler_params=pltpu.CompilerParams(
            collective_id=0, has_side_effects=True, vmem_limit_bytes=56 * 1024 * 1024
        ),
    )(
        cholesky, trial_orbitals.T, intersection_inverse, jnp.swapaxes(walkers, 1, 2), drawn, picks, parents
    )
    return (jnp.swapaxes(new_walkers, 1, 2), force_bias)


def solution(mesh):
    in_specs = (
        P("sub", "pair", None),
        P(),
        P(("grp", "pair", "rep"), None, "sub"),
        P(("grp", "pair", "rep"), None, None),
        P("grp"),
        P("grp"),
        P(("grp", "pair", "rep")),
    )
    out_specs = (P(("grp", "pair", "rep"), None, "sub"), P(("grp", "pair", "rep"), "sub"))
    return jax.shard_map(shards, mesh=mesh, in_specs=in_specs, out_specs=out_specs, check_vma=False)
```

time: 97.2 us -> 70 us (0.72)
  blocking collectives: 7.84 us -> 0 us
  Pallas kernels: 67.4 us -> 62 us
  local copies, waits for them, and re-layouts: 9.33 us -> 4.41 us
  starting transfers between devices: 3.58 us -> 0 us
  matrix products: 3.54 us -> 0 us
  other arithmetic: 4.32 us -> 2.75 us
    all_to_all x2 -> x0, blocking collectives: 7.84 us -> none  [the longest x1 3.92 us: shards(): lax.all_to_all(chosen, 'sub', split_axis=0, concat_axis=2, tiled=True)[0]]
    pallas_call x1, Pallas kernels: 67.4 us -> 62 us  [shards(): pl.pallas_call(functools.partial(step_kernel, n, rows), out_shape=(jax.Sh...]
    all_to_all x1 -> x0, starting transfers between devices: 3.58 us -> none  [shards(): lax.all_to_all(walkers, 'sub', split_axis=0, concat_axis=2, tiled=True)]
    dot_general x7 -> x0, matrix products: 3.54 us -> none  [the longest x6 2.63 us: shards(): product = jnp.dot(potential, taylor_term, preferred_element_type=F32)]
    pallas_call x1 -> x0, local copies, waits for them, and re-layouts: 2.89 us -> none  [shards(): pl.pallas_call(functools.partial(step_kernel, n), out_shape=(jax.ShapeDty...]
    unnamed x1 -> x0, other arithmetic: 2.16 us -> none
    unnamed x9 -> x3, local copies, waits for them, and re-layouts: 3.96 us -> 2.98 us
  transfers between devices with their start and end apart: 1 -> 0, of which waited for: 0 -> 0; matrix products, arithmetic and copies ran while one was open for 3% -> 0% of each run, Pallas kernels for 0% -> 0%
where the time goes in v2:
time: 70 us; the launch traced here: 69.8 us
  Pallas kernels  62 us (89%)
  local copies, waits for them, and re-layouts  4.41 us (6%)
  other arithmetic  2.75 us (4%)
    pallas_call x1, Pallas kernels, shards(): pl.pallas_call(functools.partial(step_kernel, n, rows), out_shape=(jax.Sh...  62 us
    unnamed x3, local copies, waits for them, and re-layouts  2.98 us
    reduce_sum x1, other arithmetic, shards(): jnp.sum(jnp.where(wanted[:, :, None] == places[None, None, :], noise_stre...  1.93 us

profile of v2, /device:TPU:0, one launch (start us, length us, event | category | flops | bytes accessed | tf_op | source)
XLA Modules:
  0.0 69.8 jit_solution(15933252304936167662)
XLA Ops:
  0.6 0.7 fusion.1
  1.3 0.1 compare_convert_fusion
  1.4 0.7 %reshape.57 = s32[4,2,2]{2,1,0:T(2,128)S(1)} reshape(s32[16]{0:T(128)} %param.12) | data formatting | bytes 128 | tf_op jit(solution)/shard_map/reshape | solution.py:321
  2.1 0.1 copy.13
  2.2 0.1 add.56
  2.3 0.1 iota_add_fusion
  2.4 1.9 %select_reduce_fusion.drawn = f32[8,128]{1,0:T(8,128)} fusion(f32[1024]{0:T(1024)} %param.11, s32[8,128]{1,0:T(8,128)S(1)} %iota_add_fusion), kind=kLoop, calls=%fused_computation | loop fusion | flops 3144704 | bytes 12288 | tf_op jit(solution)/shard_map/reduce_sum | solution.py:325
  4.3 0.6 broadcast_in_dim.16.picks
  4.9 62.0 %shard_map.86 = (bf16[2,96,640]{2,1,0:T(8,128)(2,1)}, f32[2,128]{1,0:T(2,128)}) custom-call(bf16[128,160,640]{2,1,0:T(8,128)(2,1)} %chol.1, bf16[192,640]{1,0:T(8,128)(2,1)} %bitcast.7, bf16[2,192,192]{2,1,0:T(8,128)(2,1)} %inverse.1, bf16[2,96,640]{2,1,0:T(8,128)(2,1)} %bitcast.8, f32[8,128]{1,0:T(8,128)} %select_reduce_fusion.drawn, ...), custom_call_target="tpu_custom_call" | custom-call | tf_op jit(solution)/shard_map/pallas_call | solution.py:337
  66.9 1.7 %copy.16 = bf16[2,640,96]{1,2,0:T(8,128)(2,1)} copy(bf16[2,640,96]{1,2,0:T(8,128)(2,1)} %bitcast.9) | data formatting | bytes 491520
  68.6 1.2 %copy.17 = f32[2,128]{1,0:T(2,128)} copy(f32[2,128]{1,0:T(2,128)} %get-tuple-element.9) | data formatting | bytes 2048
  (2 shorter events, 0.0 us)

commit v3 on v2

--- a/solution.py
+++ b/solution.py
@@ -20,10 +20,10 @@
 
 
 def step_kernel(
-    n, rows, chol, trial, inverse, walkers, drawn, picks, parents,
+    n, rows, chol, trial, inverse, walkers, noise, offsets, parents,
     walkers_out, bias_out,
     cbuf, wfirst, mixed, mixbuf, wbuf, rbuf, ybuf, ebuf, fbsend, fbbuf, fpad, kron, tmp, keep, psend, precv,
-    pfin, pot, xbuf, xsend, done, obuf,
+    pfin, pot, xbuf, xsend, done, obuf, picks, window,
     csem, ssem, msem, xsem, hsem, rsem, fsem, qsem, psem,
 ):
     a = lax.axis_index("pair")
@@ -52,6 +52,11 @@
             src_ref=src, dst_ref=dst, send_sem=sems.at[(0,) + place], recv_sem=sems.at[(1,) + place],
             device_id=target, device_id_type=MESH,
         )
+
+    spots = lax.broadcasted_iota(jnp.int32, (GROUP, LANES), 1)
+    for k in range(2):
+        column = lax.rem(parents[k], 2) * n + lax.div(parents[k], 2)
+        picks[k] = jnp.where(spots == column, 1.0, 0.0).astype(BF16)
 
     barrier = pltpu.get_barrier_semaphore()
     pl.semaphore_signal(barrier, inc=1, device_id=sibling, device_id_type=MESH)
@@ -99,6 +104,26 @@
             copy.start()
     mixbuf[s, a] = mixed[a]
 
+    rep, rep_size = lax.axis_index("rep"), lax.axis_size("rep")
+    low = jnp.zeros((walks, 2 * LANES), jnp.int32)
+    number = lax.broadcasted_iota(jnp.int32, (walks, 2 * LANES), 0)
+    for b in range(n):
+        for k in range(2):
+            place = offsets[(b * rep_size + rep) * 2 + k] + s * count
+            row = lax.div(place, LANES)
+            w = k * n + b
+            window[w : w + 1, 0:LANES] = noise[pl.ds(row, 1), :]
+            after = jnp.minimum(row + 1, noise.shape[0] - 1)
+            window[w : w + 1, LANES:] = noise[pl.ds(after, 1), :]
+            low = jnp.where(number == w, lax.rem(place, LANES), low)
+    seen = window[...]
+    amount = 1
+    while amount < LANES:
+        turned = jnp.concatenate([seen[:, amount:], seen[:, :amount]], axis=1)
+        seen = jnp.where(lax.rem(lax.div(low, amount), 2) == 1, turned, seen)
+        amount *= 2
+    window[...] = seen
+
     ybuf[...] = jnp.zeros_like(ybuf)
     fpad[...] = jnp.zeros_like(fpad)
     ebuf[...] = jnp.where(
@@ -138,7 +163,7 @@
             copy.wait_recv()
             forward.start()
 
-    tile = max(GROUP, min(deep, 65536 // wide) // GROUP * GROUP)
+    tile = max(GROUP, min(deep, 131072 // wide) // GROUP * GROUP)
     share = tile // GROUP
 
     def bias_group(j):
@@ -188,7 +213,7 @@
     for copy in pick_copies + bias_copies:
         copy.wait_recv()
     total = jnp.sum(fbbuf[...], axis=0)
-    fpad[0:walks, :] = drawn[...] - total
+    fpad[0:walks, :] = window[:, 0:LANES] - total
     fields = fpad[...].astype(BF16)
 
     step = 8 * GROUP
@@ -258,7 +283,13 @@
     child_copy = remote(xsend, xbuf.at[s], ssem, (1,), sibling)
     child_copy.start()
     child_copy.wait_recv()
-    term = xbuf[...].reshape(electrons, orbitals)
+    eye = jnp.where(
+        lax.broadcasted_iota(jnp.int32, (electrons, electrons), 0)
+        == lax.broadcasted_iota(jnp.int32, (electrons, electrons), 1), 1.0, 0.0
+    ).astype(BF16)
+    term = lax.dot_general(
+        xbuf[...].reshape(electrons, orbitals), eye, (((0,), (0,)), ((), ())), preferred_element_type=F32
+    ).astype(BF16)
     summed = term.astype(F32)
 
     @pl.loop(0, groups)
@@ -267,14 +298,16 @@
             pot_copy(d, b, j).wait_recv()
 
     for degree in range(1, TAYLOR + 1):
-        product = lax.dot_general(
-            term, pot[...].reshape(n * padded, orbitals), NT, preferred_element_type=F32
+        product = jnp.dot(
+            pot[...].reshape(n * padded, orbitals), term, preferred_element_type=F32
         )
         term = (product / jnp.float32(degree)).astype(BF16)
         if padded != rows:
-            term = lax.dot_general(term, layout, NT, preferred_element_type=F32).astype(BF16)
+            term = jnp.dot(layout, term, preferred_element_type=F32).astype(BF16)
         summed = summed + term.astype(F32)
-    done[...] = summed.astype(BF16).reshape(done.shape)
+    done[...] = lax.dot_general(
+        eye, summed.astype(BF16), NT, preferred_element_type=F32
+    ).astype(BF16).reshape(done.shape)
     last_copy = remote(done.at[1 - s], obuf.at[s], ssem, (2,), sibling)
     last_copy.start()
     obuf[s] = done[s]
@@ -306,29 +339,13 @@
     walk_count, _, half = walkers.shape
     electrons = trial_orbitals.shape[1]
     n = lax.axis_size("pair")
-    rep_size = lax.axis_size("rep")
-    rep_index = lax.axis_index("rep")
-    sub_index = lax.axis_index("sub")
-    assert walk_count == 2 and lax.axis_size("sub") == 2
+    assert walk_count == 2 and lax.axis_size("sub") == 2 and count == LANES
     padded = -(-rows // GROUP) * GROUP
     groups = padded // GROUP
     walks = walk_count * n
     wide, deep = walks * GROUP, count * GROUP
-    split = max(1, groups // 2)
     if padded != rows:
         cholesky = jnp.pad(cholesky, ((0, 0), (0, padded - rows), (0, 0)))
-
-    offsets_grid = offsets.reshape(n, rep_size, walk_count)
-    row_offsets = lax.dynamic_index_in_dim(offsets_grid, rep_index, 1, False).T.reshape(-1)
-    wanted = row_offsets[:, None] + sub_index * count + jnp.arange(count, dtype=jnp.int32)[None, :]
-    places = jnp.arange(noise_stream.shape[0], dtype=jnp.int32)
-    drawn = jnp.sum(
-        jnp.where(wanted[:, :, None] == places[None, None, :], noise_stream[None, None, :], 0.0), axis=2
-    )
-
-    columns = (parents % walk_count) * n + parents // walk_count
-    picks = (columns[:, None] == jnp.arange(LANES, dtype=jnp.int32)[None, :]).astype(BF16)
-    picks = jnp.broadcast_to(picks[:, None, :], (walk_count, GROUP, LANES))
 
     vmem = pl.BlockSpec(memory_space=pltpu.VMEM)
     smem = pl.BlockSpec(memory_space=pltpu.SMEM)
@@ -340,7 +357,7 @@
             jax.ShapeDtypeStruct((walk_count, half, orbitals), BF16),
             jax.ShapeDtypeStruct((walk_count, count), F32),
         ),
-        in_specs=[hbm, vmem, vmem, vmem, vmem, vmem, smem],
+        in_specs=[hbm, vmem, vmem, vmem, vmem, smem, smem],
         out_specs=(vmem, vmem),
         scratch_shapes=[
             pltpu.VMEM((groups, count, GROUP, orbitals), BF16),
@@ -365,6 +382,8 @@
             pltpu.VMEM((half, orbitals), BF16),
             pltpu.VMEM((2, half, orbitals), BF16),
             pltpu.VMEM((2, half, orbitals), BF16),
+            pltpu.VMEM((walk_count, GROUP, LANES), BF16),
+            pltpu.VMEM((walks, 2 * LANES), F32),
             dma((groups,)),
             dma((2, 3)),
             dma((2, 2, n)),
@@ -376,10 +395,11 @@
             dma((2, n, groups)),
         ],
         compiler_params=pltpu.CompilerParams(
-            collective_id=0, has_side_effects=True, vmem_limit_bytes=56 * 1024 * 1024
+            collective_id=0, has_side_effects=True, vmem_limit_bytes=44 * 1024 * 1024
         ),
     )(
-        cholesky, trial_orbitals.T, intersection_inverse, jnp.swapaxes(walkers, 1, 2), drawn, picks, parents
+        cholesky, trial_orbitals.T, intersection_inverse, jnp.swapaxes(walkers, 1, 2),
+        noise_stream.reshape(-1, LANES), offsets, parents,
     )
     return (jnp.swapaxes(new_walkers, 1, 2), force_bias)
 

time: 70 us -> 66.6 us (0.951)
  other arithmetic: 2.75 us -> 0 us
  Pallas kernels: 62 us -> 59.6 us
  local copies, waits for them, and re-layouts: 4.41 us -> 6.06 us
    unnamed x3 -> x14, local copies, waits for them, and re-layouts: 2.98 us -> 6.06 us
    pallas_call x1, Pallas kernels: 62 us -> 59.6 us  [shards(): pl.pallas_call(functools.partial(step_kernel, n, rows), out_shape=(jax.Sh...]
    reduce_sum x1 -> x0, other arithmetic: 1.93 us -> none  [shards(): jnp.sum(jnp.where(wanted[:, :, None] == places[None, None, :], noise_stre...]
    add x3 -> x0, other arithmetic: 0.75 us -> none  [the longest x1 0.67 us: shards(): columns = parents % walk_count * n + parents // walk_count]
    reshape x1 -> x0, local copies, waits for them, and re-layouts: 0.74 us -> none  [shards(): offsets_grid = offsets.reshape(n, rep_size, walk_count)]
where the time goes in v3:
time: 66.6 us; the launch traced here: 66.3 us
  Pallas kernels  59.6 us (89%)
  local copies, waits for them, and re-layouts  6.06 us (9%)
    pallas_call x1, Pallas kernels, shards(): pl.pallas_call(functools.partial(step_kernel, n, rows), out_shape=(jax.Sh...  59.6 us
    unnamed x14, local copies, waits for them, and re-layouts  6.06 us

profile of v3, /device:TPU:0, one launch (start us, length us, event | category | flops | bytes accessed | tf_op | source)
XLA Modules:
  0.0 66.3 jit_solution(7914325751302148395)
XLA Ops:
  0.6 0.0 copy-start
  0.6 0.9 %copy-done = bf16[640,192]{0,1:T(8,128)(2,1)S(1)} copy-done((bf16[640,192]{0,1:T(8,128)(2,1)S(1)}, bf16[640,192]{0,1:T(8,128)(2,1)}, u32[]{:S(2)}) %copy-start) | copy-done | bytes 245784
  1.6 0.0 copy-start.1
  1.6 0.9 %copy-done.1 = bf16[2,640,96]{1,2,0:T(8,128)(2,1)S(1)} copy-done((bf16[2,640,96]{1,2,0:T(8,128)(2,1)S(1)}, bf16[2,640,96]{1,2,0:T(8,128)(2,1)}, u32[]{:S(2)}) %copy-start.1) | copy-done | bytes 245784
  2.5 0.0 copy-start.2
  2.5 0.9 %copy-done.2 = bf16[2,192,192]{2,1,0:T(8,128)(2,1)S(1)} copy-done((bf16[2,192,192]{2,1,0:T(8,128)(2,1)S(1)}, bf16[2,192,192]{2,1,0:T(8,128)(2,1)}, u32[]{:S(2)}) %copy-start.2) | copy-done | bytes 147480
  3.4 0.0 copy-start.3
  3.5 0.7 %copy-done.3 = f32[1024]{0:T(1024)S(1)} copy-done((f32[1024]{0:T(1024)S(1)}, f32[1024]{0:T(1024)}, u32[]{:S(2)}) %copy-start.3) | copy-done | bytes 4120
  4.1 0.0 copy-start.4
  4.1 0.7 copy-done.4
  4.8 0.0 copy-start.5
  4.8 0.7 copy-done.5
  5.4 59.6 %shard_map.86 = (bf16[2,96,640]{2,1,0:T(8,128)(2,1)S(1)}, f32[2,128]{1,0:T(2,128)S(1)}) custom-call(bf16[128,160,640]{2,1,0:T(8,128)(2,1)} %chol.1, bf16[192,640]{1,0:T(8,128)(2,1)S(1)} %bitcast.5, bf16[2,192,192]{2,1,0:T(8,128)(2,1)S(1)} %copy-done.2, bf16[2,96,640]{2,1,0:T(8,128)(2,1)S(1)} %bitcast.6, f32[8,128]{1,0:T(8,128)S(1)} %bitcast.7, ...), custom_call_target="tpu_custom_call" | custom-call | tf_op jit(solution)/shard_map/pallas_call | solution.py:354
  65.1 0.7 %copy.11 = bf16[2,640,96]{1,2,0:T(8,128)(2,1)} copy(bf16[2,640,96]{1,2,0:T(8,128)(2,1)S(1)} %bitcast.4) | data formatting | bytes 491520
  65.7 0.6 copy.12
Async XLA Ops:
  0.6 0.9 %copy-start = (bf16[640,192]{0,1:T(8,128)(2,1)S(1)}, bf16[640,192]{0,1:T(8,128)(2,1)}, u32[]{:S(2)}) copy-start(bf16[640,192]{0,1:T(8,128)(2,1)} %param.8) | copy-start | bytes 737284
  1.6 0.9 %copy-start.1 = (bf16[2,640,96]{1,2,0:T(8,128)(2,1)S(1)}, bf16[2,640,96]{1,2,0:T(8,128)(2,1)}, u32[]{:S(2)}) copy-start(bf16[2,640,96]{1,2,0:T(8,128)(2,1)} %param.9) | copy-start | bytes 737284
  2.5 0.9 %copy-start.2 = (bf16[2,192,192]{2,1,0:T(8,128)(2,1)S(1)}, bf16[2,192,192]{2,1,0:T(8,128)(2,1)}, u32[]{:S(2)}) copy-start(bf16[2,192,192]{2,1,0:T(8,128)(2,1)} %inverse.1) | copy-start | bytes 442372
  3.4 0.7 %copy-start.3 = (f32[1024]{0:T(1024)S(1)}, f32[1024]{0:T(1024)}, u32[]{:S(2)}) copy-start(f32[1024]{0:T(1024)} %param.11) | copy-start | bytes 12292
  4.1 0.7 copy-start.4
  4.8 0.7 copy-start.5

commit v4 on v3

--- a/solution.py
+++ b/solution.py
@@ -20,31 +20,49 @@
 
 
 def step_kernel(
-    n, rows, chol, trial, inverse, walkers, noise, offsets, parents,
+    n, ways, rows, chol, trial_in, inverse_in, walkers_in, noise_in, offsets, parents,
     walkers_out, bias_out,
     cbuf, wfirst, mixed, mixbuf, wbuf, rbuf, ybuf, ebuf, fbsend, fbbuf, fpad, kron, tmp, keep, psend, precv,
-    pfin, pot, xbuf, xsend, done, obuf, picks, window,
-    csem, ssem, msem, xsem, hsem, rsem, fsem, qsem, psem,
+    pfin, pot, xbuf, xsend, done, obuf, picks, window, trial, inverse, noise,
+    csem, ssem, msem, xsem, hsem, rsem, fsem, qsem, psem, isem,
 ):
     a = lax.axis_index("pair")
     s = lax.axis_index("sub")
     groups, count = cbuf.shape[0], cbuf.shape[1]
     electrons, orbitals = trial.shape
-    padded = groups * GROUP
-    walks = 2 * n
+    every = n * ways
+    q = lax.axis_index("rep") if ways > 1 else 0
+    me = q * n + a
+    span = groups * GROUP
+    padded = span * ways
+    walks = 2 * every
     wide = walks * GROUP
     deep = count * GROUP
 
     def chol_copy(j):
         return pltpu.make_async_copy(
-            chol.at[:, pl.ds(pl.multiple_of(j * GROUP, GROUP), GROUP), :], cbuf.at[j], csem.at[j]
+            chol.at[:, pl.ds(pl.multiple_of(q * span + j * GROUP, GROUP), GROUP), :],
+            cbuf.at[j], csem.at[j],
         )
+
+    own_walkers = pl.ds(2 * a, 2)
+    loads = [
+        pltpu.make_async_copy(src, dst, isem.at[i])
+        for i, (src, dst) in enumerate(
+            [(walkers_in, wbuf.at[own_walkers]), (inverse_in, inverse), (noise_in, noise), (trial_in, trial)]
+        )
+    ]
+    for load in loads:
+        load.start()
 
     @pl.loop(0, groups)
     def _(j):
         chol_copy(j).start()
 
-    peers = [(d, lax.rem(a + d, n)) for d in range(1, n)]
+    peers = [(d, lax.rem(me + d, every)) for d in range(1, every)]
+
+    def holder(c):
+        return {"pair": lax.rem(c, n), "rep": lax.div(c, n)} if ways > 1 else {"pair": c}
     sibling = {"sub": 1 - s}
 
     def remote(src, dst, sems, place, target):
@@ -55,23 +73,25 @@
 
     spots = lax.broadcasted_iota(jnp.int32, (GROUP, LANES), 1)
     for k in range(2):
-        column = lax.rem(parents[k], 2) * n + lax.div(parents[k], 2)
+        column = lax.rem(parents[k], 2) * every + q * n + lax.div(parents[k], 2)
         picks[k] = jnp.where(spots == column, 1.0, 0.0).astype(BF16)
 
     barrier = pltpu.get_barrier_semaphore()
     pl.semaphore_signal(barrier, inc=1, device_id=sibling, device_id_type=MESH)
-    for _, b in peers:
-        pl.semaphore_signal(barrier, inc=1, device_id={"pair": b}, device_id_type=MESH)
-    pl.semaphore_wait(barrier, n)
-
-    first_copy = remote(walkers.at[1 - s], wfirst.at[s], ssem, (0,), sibling)
+    for _, c in peers:
+        pl.semaphore_signal(barrier, inc=1, device_id=holder(c), device_id_type=MESH)
+    loads[0].wait()
+    pl.semaphore_wait(barrier, every)
+
+    first_copy = remote(wbuf.at[2 * a + 1 - s], wfirst.at[s], ssem, (0,), sibling)
     first_copy.start()
-    pick_copies = [remote(picks, rbuf.at[:, a], rsem, (d,), {"pair": b}) for d, b in peers]
+    pick_copies = [remote(picks, rbuf.at[:, me], rsem, (d,), holder(c)) for d, c in peers]
     for copy in pick_copies:
         copy.start()
-    wfirst[s] = walkers[s]
-    wbuf[pl.ds(2 * a, 2)] = walkers[...]
-    rbuf[:, a] = picks[...]
+    wfirst[s] = wbuf[2 * a + s]
+    rbuf[:, me] = picks[...]
+    loads[1].wait()
+    loads[2].wait()
     if padded != rows:
         spot = lax.broadcasted_iota(jnp.int32, (orbitals, n * padded), 1)
         spot = jnp.where(spot % padded < rows, spot // padded * rows + spot % padded, -1)
@@ -84,34 +104,40 @@
         start = jnp.dot(start, layout, preferred_element_type=F32).astype(BF16)
     mixed[...] = lax.dot_general(
         start, inverse[s], (((0,), (0,)), ((), ())), preferred_element_type=F32
-    ).astype(BF16).reshape(n, padded, electrons)
+    ).astype(BF16).reshape(n, ways, span, electrons)
 
     split = max(1, groups // 2)
     parts = [pl.ds(0, split * GROUP), pl.ds(split * GROUP, (groups - split) * GROUP)]
     mixed_copies = [
-        [remote(mixed.at[b, part], mixbuf.at[s, a, part], msem, (h, d), {"pair": b}) for d, b in peers]
+        [
+            remote(
+                mixed.at[lax.rem(c, n), lax.div(c, n), part], mixbuf.at[s, me, part], msem, (h, d), holder(c)
+            )
+            for d, c in peers
+        ]
         for h, part in enumerate(parts)
     ]
     across_copies = [
         [
-            remote(mixbuf.at[s, b, part], mixbuf.at[s, b, part], xsem, (h, d), sibling)
-            for d, b in [(d, lax.rem(a + n - d, n)) for d in range(n)]
+            remote(mixbuf.at[s, c, part], mixbuf.at[s, c, part], xsem, (h, d), sibling)
+            for d, c in [(d, lax.rem(me + every - d, every)) for d in range(every)]
         ]
         for h, part in enumerate(parts)
     ]
     for h in range(2):
         for copy in mixed_copies[h]:
             copy.start()
-    mixbuf[s, a] = mixed[a]
+    mixbuf[s, me] = mixed[a, q]
 
     rep, rep_size = lax.axis_index("rep"), lax.axis_size("rep")
     low = jnp.zeros((walks, 2 * LANES), jnp.int32)
     number = lax.broadcasted_iota(jnp.int32, (walks, 2 * LANES), 0)
-    for b in range(n):
+    for c in range(every):
         for k in range(2):
-            place = offsets[(b * rep_size + rep) * 2 + k] + s * count
+            home = c // n if ways > 1 else rep
+            place = offsets[(c % n * rep_size + home) * 2 + k] + s * count
             row = lax.div(place, LANES)
-            w = k * n + b
+            w = k * every + c
             window[w : w + 1, 0:LANES] = noise[pl.ds(row, 1), :]
             after = jnp.minimum(row + 1, noise.shape[0] - 1)
             window[w : w + 1, LANES:] = noise[pl.ds(after, 1), :]
@@ -163,7 +189,7 @@
             copy.wait_recv()
             forward.start()
 
-    tile = max(GROUP, min(deep, 131072 // wide) // GROUP * GROUP)
+    tile = max(GROUP, min(deep, 262144 // wide) // GROUP * GROUP)
     share = tile // GROUP
 
     def bias_group(j):
@@ -183,6 +209,7 @@
     for copy in across_copies[0]:
         copy.wait_recv()
     chain_step(0)
+    loads[3].wait()
     pl.loop(0, split - 1)(bias_group)
     pass_across(1)
     pl.loop(split - 1, split)(bias_group)
@@ -206,8 +233,8 @@
         adder, traced, NT, preferred_element_type=F32, precision=lax.Precision.HIGHEST
     )
     fbsend[...] = partial
-    fbbuf[a] = partial
-    bias_copies = [remote(fbsend, fbbuf.at[a], fsem, (d,), {"pair": b}) for d, b in peers]
+    fbbuf[me] = partial
+    bias_copies = [remote(fbsend, fbbuf.at[me], fsem, (d,), holder(c)) for d, c in peers]
     for copy in bias_copies:
         copy.start()
     for copy in pick_copies + bias_copies:
@@ -216,7 +243,8 @@
     fpad[0:walks, :] = window[:, 0:LANES] - total
     fields = fpad[...].astype(BF16)
 
-    step = 8 * GROUP
+    some = min(16, walks)
+    step = some * GROUP
     chunks = wide // step
 
     @pl.loop(0, chunks)
@@ -224,8 +252,8 @@
         if chunks == 1:
             chosen = rbuf[...].reshape(step, LANES)
         else:
-            per = n // 8
-            chosen = rbuf[c // per, pl.ds(lax.rem(c, per) * 8, 8)].reshape(step, LANES)
+            per = every // some
+            chosen = rbuf[c // per, pl.ds(lax.rem(c, per) * some, some)].reshape(step, LANES)
         spread = jnp.dot(chosen, fields, preferred_element_type=F32).astype(BF16)
         full = jnp.dot(spread, ebuf[...], preferred_element_type=F32)
         diagonal = (
@@ -237,9 +265,9 @@
     def part_copy(j):
         return remote(psend.at[j], precv.at[j], qsem, (j,), sibling)
 
-    def pot_copy(d, b, j):
+    def pot_copy(d, c, j):
         at = pl.ds(pl.multiple_of(j * GROUP, GROUP), GROUP)
-        return remote(pfin.at[b, at], pot.at[a, at], psem, (d, j), {"pair": b})
+        return remote(pfin.at[c, at], pot.at[a, q, at], psem, (d, j), holder(c))
 
     def finish(j):
         part_copy(j).wait_recv()
@@ -251,30 +279,30 @@
     def potential_group(j):
         @pl.loop(0, chunks)
         def _(c):
-            tmp[pl.ds(c * 8, 8)] = jnp.dot(
+            tmp[pl.ds(c * some, some)] = jnp.dot(
                 kron[c], cbuf[j].reshape(deep, orbitals), preferred_element_type=F32
-            ).reshape(8, GROUP, orbitals)
-
-        psend[j] = tmp[pl.ds((1 - s) * n, n)].astype(BF16)
+            ).reshape(some, GROUP, orbitals)
+
+        psend[j] = tmp[pl.ds((1 - s) * every, every)].astype(BF16)
         part_copy(j).start()
-        keep[j] = tmp[pl.ds(s * n, n)]
+        keep[j] = tmp[pl.ds(s * every, every)]
 
         @pl.when(j > 0)
         def _():
             finish(j - 1)
 
-    early = min(3, groups)
+    early = min(2, groups)
     pl.loop(0, early)(potential_group)
     if n > 2:
         chain_step(2)
     pl.loop(early, groups)(potential_group)
     finish(groups - 1)
-    pot[a] = pfin[a]
+    pot[a, q] = pfin[me]
 
     fbsend_rows = fpad.at[0:walks]
     fbsend_rows[...] = total
     for k in range(2):
-        bias_out[k : k + 1, :] = fpad[pl.ds(k * n + a, 1), :]
+        bias_out[k : k + 1, :] = fpad[pl.ds(k * every + me, 1), :]
 
     for t in range(3, n):
         chain_step(t)
@@ -334,15 +362,31 @@
     walkers_out[...] = obuf[...]
 
 
+def hand_over(walkers, bias, walkers_out, bias_out, sems):
+    copies = [
+        pltpu.make_async_copy(walkers, walkers_out, sems.at[0]),
+        pltpu.make_async_copy(bias, bias_out, sems.at[1]),
+    ]
+    for copy in copies:
+        copy.start()
+    for copy in copies:
+        copy.wait()
+
+
 def shards(cholesky, trial_orbitals, walkers, intersection_inverse, noise_stream, offsets, parents):
     count, rows, orbitals = cholesky.shape
     walk_count, _, half = walkers.shape
     electrons = trial_orbitals.shape[1]
     n = lax.axis_size("pair")
     assert walk_count == 2 and lax.axis_size("sub") == 2 and count == LANES
-    padded = -(-rows // GROUP) * GROUP
-    groups = padded // GROUP
-    walks = walk_count * n
+    ways = lax.axis_size("rep")
+    if walk_count * n * ways * GROUP > 1024:
+        ways = 1
+    every = n * ways
+    groups = -(-rows // (GROUP * ways))
+    span = groups * GROUP
+    padded = span * ways
+    walks = walk_count * every
     wide, deep = walks * GROUP, count * GROUP
     if padded != rows:
         cholesky = jnp.pad(cholesky, ((0, 0), (0, padded - rows), (0, 0)))
@@ -352,55 +396,70 @@
     hbm = pl.BlockSpec(memory_space=pl.ANY)
     dma = pltpu.SemaphoreType.DMA
     new_walkers, force_bias = pl.pallas_call(
-        functools.partial(step_kernel, n, rows),
+        functools.partial(step_kernel, n, ways, rows),
         out_shape=(
             jax.ShapeDtypeStruct((walk_count, half, orbitals), BF16),
             jax.ShapeDtypeStruct((walk_count, count), F32),
         ),
-        in_specs=[hbm, vmem, vmem, vmem, vmem, smem, smem],
+        in_specs=[hbm, hbm, hbm, hbm, hbm, smem, smem],
         out_specs=(vmem, vmem),
         scratch_shapes=[
             pltpu.VMEM((groups, count, GROUP, orbitals), BF16),
             pltpu.VMEM((2, half, orbitals), BF16),
-            pltpu.VMEM((n, padded, electrons), BF16),
-            pltpu.VMEM((2, n, padded, electrons), BF16),
-            pltpu.VMEM((walks, half, orbitals), BF16),
-            pltpu.VMEM((2, n, GROUP, LANES), BF16),
+            pltpu.VMEM((n, ways, span, electrons), BF16),
+            pltpu.VMEM((2, every, span, electrons), BF16),
+            pltpu.VMEM((walk_count * n, half, orbitals), BF16),
+            pltpu.VMEM((2, every, GROUP, LANES), BF16),
             pltpu.VMEM((deep, wide), F32),
             pltpu.VMEM((count, deep), BF16),
             pltpu.VMEM((walks, count), F32),
-            pltpu.VMEM((n, walks, count), F32),
+            pltpu.VMEM((every, walks, count), F32),
             pltpu.VMEM((LANES, count), F32),
-            pltpu.VMEM((wide // (8 * GROUP), 8 * GROUP, deep), BF16),
+            pltpu.VMEM((walks // min(16, walks), min(16, walks) * GROUP, deep), BF16),
             pltpu.VMEM((walks, GROUP, orbitals), F32),
-            pltpu.VMEM((groups, n, GROUP, orbitals), F32),
-            pltpu.VMEM((groups, n, GROUP, orbitals), BF16),
-            pltpu.VMEM((groups, n, GROUP, orbitals), BF16),
-            pltpu.VMEM((n, padded, orbitals), BF16),
-            pltpu.VMEM((n, padded, orbitals), BF16),
+            pltpu.VMEM((groups, every, GROUP, orbitals), F32),
+            pltpu.VMEM((groups, every, GROUP, orbitals), BF16),
+            pltpu.VMEM((groups, every, GROUP, orbitals), BF16),
+            pltpu.VMEM((every, span, orbitals), BF16),
+            pltpu.VMEM((n, ways, span, orbitals), BF16),
             pltpu.VMEM((2, half, orbitals), BF16),
             pltpu.VMEM((half, orbitals), BF16),
             pltpu.VMEM((2, half, orbitals), BF16),
             pltpu.VMEM((2, half, orbitals), BF16),
             pltpu.VMEM((walk_count, GROUP, LANES), BF16),
             pltpu.VMEM((walks, 2 * LANES), F32),
+            pltpu.VMEM((electrons, orbitals), BF16),
+            pltpu.VMEM((walk_count, electrons, electrons), BF16),
+            pltpu.VMEM((noise_stream.shape[0] // LANES, LANES), F32),
             dma((groups,)),
             dma((2, 3)),
+            dma((2, 2, every)),
+            dma((2, 2, every)),
             dma((2, 2, n)),
-            dma((2, 2, n)),
-            dma((2, 2, n)),
-            dma((2, n)),
-            dma((2, n)),
+            dma((2, every)),
+            dma((2, every)),
             dma((2, groups)),
-            dma((2, n, groups)),
+            dma((2, every, groups)),
+            dma((4,)),
         ],
         compiler_params=pltpu.CompilerParams(
-            collective_id=0, has_side_effects=True, vmem_limit_bytes=44 * 1024 * 1024
+            collective_id=0, has_side_effects=True, vmem_limit_bytes=58 * 1024 * 1024
         ),
     )(
         cholesky, trial_orbitals.T, intersection_inverse, jnp.swapaxes(walkers, 1, 2),
         noise_stream.reshape(-1, LANES), offsets, parents,
     )
+    new_walkers, force_bias = pl.pallas_call(
+        hand_over,
+        out_shape=(
+            jax.ShapeDtypeStruct(new_walkers.shape, BF16),
+            jax.ShapeDtypeStruct(force_bias.shape, F32),
+        ),
+        in_specs=[hbm, hbm],
+        out_specs=(hbm, hbm),
+        scratch_shapes=[dma((2,))],
+        compiler_params=pltpu.CompilerParams(vmem_limit_bytes=58 * 1024 * 1024),
+    )(new_walkers, force_bias)
     return (jnp.swapaxes(new_walkers, 1, 2), force_bias)
 
 

time: 66.6 us -> 70.8 us (1.063)
  Pallas kernels: 59.6 us -> 70 us
  local copies, waits for them, and re-layouts: 6.06 us -> 0 us
    pallas_call x1 -> x2, Pallas kernels: 59.6 us -> 70 us  [the longest x1 61.4 us: shards(): pl.pallas_call(functools.partial(step_kernel, n, ways, rows), out_shape=(...]
    unnamed x14 -> x0, local copies, waits for them, and re-layouts: 6.06 us -> none
where the time goes in v4:
time: 70.8 us; the launch traced here: 70.7 us
  Pallas kernels  70 us (99%)
    pallas_call x1, Pallas kernels, shards(): pl.pallas_call(functools.partial(step_kernel, n, ways, rows), out_shape=(...  61.4 us
    pallas_call x1, Pallas kernels, shards(): pl.pallas_call(hand_over, out_shape=(jax.ShapeDtypeStruct(new_walkers.sha...  8.6 us

profile of v4, /device:TPU:0, one launch (start us, length us, event | category | flops | bytes accessed | tf_op | source)
XLA Modules:
  0.0 70.7 jit_solution(12480040969902974880)
XLA Ops:
  0.6 61.4 %shard_map.86 = (bf16[2,96,640]{2,1,0:T(8,128)(2,1)}, f32[2,128]{1,0:T(2,128)}) custom-call(bf16[128,160,640]{2,1,0:T(8,128)(2,1)} %chol.1, bf16[192,640]{1,0:T(8,128)(2,1)} %bitcast.4, bf16[2,192,192]{2,1,0:T(8,128)(2,1)} %inverse_in.1, bf16[2,96,640]{2,1,0:T(8,128)(2,1)} %bitcast.5, f32[8,128]{1,0:T(8,128)} %bitcast.6, s32[16]{0:T(128)} %offsets.1, s32[2]{0:T(128)} %parents.1), custom_call_target="tpu_custom_call" | custom-call | tf_op jit(solution)/shard_map/pallas_call | solution.py:398
  62.1 8.6 %shard_map.87 = (bf16[2,96,640]{2,1,0:T(8,128)(2,1)}, f32[2,128]{1,0:T(2,128)}) custom-call(bf16[2,96,640]{2,1,0:T(8,128)(2,1)} %get-tuple-element.6.walkers, f32[2,128]{1,0:T(2,128)} %get-tuple-element.7.bias), custom_call_target="tpu_custom_call" | custom-call | tf_op jit(solution)/shard_map/pallas_call | solution.py:452

commit v5 on v4

--- a/solution.py
+++ b/solution.py
@@ -23,7 +23,7 @@
     n, ways, rows, chol, trial_in, inverse_in, walkers_in, noise_in, offsets, parents,
     walkers_out, bias_out,
     cbuf, wfirst, mixed, mixbuf, wbuf, rbuf, ybuf, ebuf, fbsend, fbbuf, fpad, kron, tmp, keep, psend, precv,
-    pfin, pot, xbuf, xsend, done, obuf, picks, window, trial, inverse, noise,
+    pfin, pot, xbuf, xsend, done, picks, window, trial, inverse, noise,
     csem, ssem, msem, xsem, hsem, rsem, fsem, qsem, psem, isem,
 ):
     a = lax.axis_index("pair")
@@ -106,6 +106,32 @@
         start, inverse[s], (((0,), (0,)), ((), ())), preferred_element_type=F32
     ).astype(BF16).reshape(n, ways, span, electrons)
 
+    def chain_copy(way, t):
+        block = a - t if way == 0 else a + t
+        at = pl.ds(2 * block, 2)
+        return remote(wbuf.at[at], wbuf.at[at], hsem, (way, t), {"pair": a + 1 - 2 * way})
+
+    def chain_sends(way, t):
+        return (a >= t) & (a + 1 < n) if way == 0 else (a + t < n) & (a > 0)
+
+    def chain_gets(way, t):
+        return a >= t + 1 if way == 0 else a + t + 1 < n
+
+    def chain_step(t):
+        for way in range(2):
+            if t > 0:
+                @pl.when(chain_gets(way, t - 1))
+                def _():
+                    back = a - t if way == 0 else a + t
+                    at = pl.ds(2 * back, 2)
+                    remote(
+                        wbuf.at[at], wbuf.at[at], hsem, (way, t - 1), {"pair": a - 1 + 2 * way}
+                    ).wait_recv()
+            if t < n - 1:
+                @pl.when(chain_sends(way, t))
+                def _():
+                    chain_copy(way, t).start()
+
     split = max(1, groups // 2)
     parts = [pl.ds(0, split * GROUP), pl.ds(split * GROUP, (groups - split) * GROUP)]
     mixed_copies = [
@@ -127,6 +153,7 @@
     for h in range(2):
         for copy in mixed_copies[h]:
             copy.start()
+    chain_step(0)
     mixbuf[s, me] = mixed[a, q]
 
     rep, rep_size = lax.axis_index("rep"), lax.axis_size("rep")
@@ -157,32 +184,6 @@
         == lax.broadcasted_iota(jnp.int32, (count, deep), 0), 1.0, 0.0
     ).astype(BF16)
 
-    def chain_copy(way, t):
-        block = a - t if way == 0 else a + t
-        at = pl.ds(2 * block, 2)
-        return remote(wbuf.at[at], wbuf.at[at], hsem, (way, t), {"pair": a + 1 - 2 * way})
-
-    def chain_sends(way, t):
-        return (a >= t) & (a + 1 < n) if way == 0 else (a + t < n) & (a > 0)
-
-    def chain_gets(way, t):
-        return a >= t + 1 if way == 0 else a + t + 1 < n
-
-    def chain_step(t):
-        for way in range(2):
-            if t > 0:
-                @pl.when(chain_gets(way, t - 1))
-                def _():
-                    back = a - t if way == 0 else a + t
-                    at = pl.ds(2 * back, 2)
-                    remote(
-                        wbuf.at[at], wbuf.at[at], hsem, (way, t - 1), {"pair": a - 1 + 2 * way}
-                    ).wait_recv()
-            if t < n - 1:
-                @pl.when(chain_sends(way, t))
-                def _():
-                    chain_copy(way, t).start()
-
     def pass_across(h):
         across_copies[h][0].start()
         for copy, forward in zip(mixed_copies[h], across_copies[h][1:]):
@@ -208,17 +209,13 @@
     pass_across(0)
     for copy in across_copies[0]:
         copy.wait_recv()
-    chain_step(0)
     loads[3].wait()
     pl.loop(0, split - 1)(bias_group)
     pass_across(1)
     pl.loop(split - 1, split)(bias_group)
     for copy in across_copies[1]:
         copy.wait_recv()
-    late = max(split, groups - 2)
-    pl.loop(split, late)(bias_group)
-    chain_step(1)
-    pl.loop(late, groups)(bias_group)
+    pl.loop(split, groups)(bias_group)
 
     same = (
         lax.broadcasted_iota(jnp.int32, (1, GROUP, wide), 1)
@@ -237,6 +234,7 @@
     bias_copies = [remote(fbsend, fbbuf.at[me], fsem, (d,), holder(c)) for d, c in peers]
     for copy in bias_copies:
         copy.start()
+    chain_step(1)
     for copy in pick_copies + bias_copies:
         copy.wait_recv()
     total = jnp.sum(fbbuf[...], axis=0)
@@ -291,12 +289,10 @@
         def _():
             finish(j - 1)
 
-    early = min(2, groups)
-    pl.loop(0, early)(potential_group)
+    pl.loop(0, groups)(potential_group)
+    finish(groups - 1)
     if n > 2:
         chain_step(2)
-    pl.loop(early, groups)(potential_group)
-    finish(groups - 1)
     pot[a, q] = pfin[me]
 
     fbsend_rows = fpad.at[0:walks]
@@ -336,9 +332,9 @@
     done[...] = lax.dot_general(
         eye, summed.astype(BF16), NT, preferred_element_type=F32
     ).astype(BF16).reshape(done.shape)
-    last_copy = remote(done.at[1 - s], obuf.at[s], ssem, (2,), sibling)
+    last_copy = remote(done.at[1 - s], walkers_out.at[s], ssem, (2,), sibling)
     last_copy.start()
-    obuf[s] = done[s]
+    walkers_out[s] = done[s]
 
     first_copy.wait_send()
     child_copy.wait_send()
@@ -359,18 +355,6 @@
             pot_copy(d, b, j).wait_send()
 
     last_copy.wait()
-    walkers_out[...] = obuf[...]
-
-
-def hand_over(walkers, bias, walkers_out, bias_out, sems):
-    copies = [
-        pltpu.make_async_copy(walkers, walkers_out, sems.at[0]),
-        pltpu.make_async_copy(bias, bias_out, sems.at[1]),
-    ]
-    for copy in copies:
-        copy.start()
-    for copy in copies:
-        copy.wait()
 
 
 def shards(cholesky, trial_orbitals, walkers, intersection_inverse, noise_stream, offsets, parents):
@@ -425,7 +409,6 @@
             pltpu.VMEM((2, half, orbitals), BF16),
             pltpu.VMEM((half, orbitals), BF16),
             pltpu.VMEM((2, half, orbitals), BF16),
-            pltpu.VMEM((2, half, orbitals), BF16),
             pltpu.VMEM((walk_count, GROUP, LANES), BF16),
             pltpu.VMEM((walks, 2 * LANES), F32),
             pltpu.VMEM((electrons, orbitals), BF16),
@@ -449,17 +432,6 @@
         cholesky, trial_orbitals.T, intersection_inverse, jnp.swapaxes(walkers, 1, 2),
         noise_stream.reshape(-1, LANES), offsets, parents,
     )
-    new_walkers, force_bias = pl.pallas_call(
-        hand_over,
-        out_shape=(
-            jax.ShapeDtypeStruct(new_walkers.shape, BF16),
-            jax.ShapeDtypeStruct(force_bias.shape, F32),
-        ),
-        in_specs=[hbm, hbm],
-        out_specs=(hbm, hbm),
-        scratch_shapes=[dma((2,))],
-        compiler_params=pltpu.CompilerParams(vmem_limit_bytes=58 * 1024 * 1024),
-    )(new_walkers, force_bias)
     return (jnp.swapaxes(new_walkers, 1, 2), force_bias)
 
 

time: 70.8 us -> 63.7 us (0.90)
  Pallas kernels: 70 us -> 60 us
  local copies, waits for them, and re-layouts: 0 us -> 2.88 us
    pallas_call x1 -> x0, Pallas kernels: 8.6 us -> none  [shards(): pl.pallas_call(hand_over, out_shape=(jax.ShapeDtypeStruct(new_walkers.sha...]
    unnamed x0 -> x2, local copies, waits for them, and re-layouts: none -> 2.88 us
    pallas_call x1, Pallas kernels: 61.4 us -> 60 us  [shards(): pl.pallas_call(functools.partial(step_kernel, n, ways, rows), out_shape=(...]
where the time goes in v5:
time: 63.7 us; the launch traced here: 63.6 us
  Pallas kernels  60 us (94%)
  local copies, waits for them, and re-layouts  2.88 us (5%)
  between operations  0.64 us (1%)
    pallas_call x1, Pallas kernels, shards(): pl.pallas_call(functools.partial(step_kernel, n, ways, rows), out_shape=(...  60 us
    unnamed x2, local copies, waits for them, and re-layouts  2.88 us

profile of v5, /device:TPU:0, one launch (start us, length us, event | category | flops | bytes accessed | tf_op | source)
XLA Modules:
  0.0 63.6 jit_solution(17681587649891650076)
XLA Ops:
  0.6 60.0 %shard_map.86 = (bf16[2,96,640]{2,1,0:T(8,128)(2,1)}, f32[2,128]{1,0:T(2,128)}) custom-call(bf16[128,160,640]{2,1,0:T(8,128)(2,1)} %chol.1, bf16[192,640]{1,0:T(8,128)(2,1)} %bitcast.5, bf16[2,192,192]{2,1,0:T(8,128)(2,1)} %inverse_in.1, bf16[2,96,640]{2,1,0:T(8,128)(2,1)} %bitcast.6, f32[8,128]{1,0:T(8,128)} %bitcast.7, s32[16]{0:T(128)} %offsets.1, s32[2]{0:T(128)} %parents.1), custom_call_target="tpu_custom_call" | custom-call | tf_op jit(solution)/shard_map/pallas_call | solution.py:382
  60.7 1.7 %copy.11 = bf16[2,640,96]{1,2,0:T(8,128)(2,1)} copy(bf16[2,640,96]{1,2,0:T(8,128)(2,1)} %bitcast.4) | data formatting | bytes 491520
  62.3 1.2 %copy.12 = f32[2,128]{1,0:T(2,128)} copy(f32[2,128]{1,0:T(2,128)} %get-tuple-element.9) | data formatting | bytes 2048

commit v6 on v5

--- a/solution.py
+++ b/solution.py
@@ -17,6 +17,19 @@
 F32 = jnp.float32
 BF16 = jnp.bfloat16
 NT = (((1,), (1,)), ((), ()))
+
+
+def mixed_rows(groups, electrons):
+    split = max(1, groups // 2)
+    packed = electrons == LANES + LANES // 2
+    places, row, starts = [], 0, []
+    for low, high in ((0, split), (split, groups)):
+        starts.append(row)
+        tails = row + (high - low) * GROUP
+        for i in range(high - low):
+            places.append((row + i * GROUP, tails + i // 2 * GROUP, i % 2))
+        row = tails + (-(-(high - low) // 2) * GROUP if packed else 0)
+    return places, starts[1], row, packed, LANES if packed else electrons
 
 
 def step_kernel(
@@ -102,9 +115,20 @@
     start = wfirst[...].reshape(electrons, orbitals)
     if padded != rows:
         start = jnp.dot(start, layout, preferred_element_type=F32).astype(BF16)
-    mixed[...] = lax.dot_general(
+    product = lax.dot_general(
         start, inverse[s], (((0,), (0,)), ((), ())), preferred_element_type=F32
     ).astype(BF16).reshape(n, ways, span, electrons)
+    places, cut, sent, packed, width = mixed_rows(groups, electrons)
+    for j, (first, tail, second) in enumerate(places):
+        rows_of = product[:, :, j * GROUP : (j + 1) * GROUP, :]
+        mixed[:, :, first : first + GROUP, :] = rows_of[..., :width]
+        if packed and not second:
+            beside = (
+                product[:, :, (j + 1) * GROUP : (j + 2) * GROUP, width:]
+                if j + 1 < groups and places[j + 1][2]
+                else jnp.zeros_like(rows_of[..., width:])
+            )
+            mixed[:, :, tail : tail + GROUP, :] = jnp.concatenate([rows_of[..., width:], beside], axis=-1)
 
     def chain_copy(way, t):
         block = a - t if way == 0 else a + t
@@ -133,7 +157,7 @@
                     chain_copy(way, t).start()
 
     split = max(1, groups // 2)
-    parts = [pl.ds(0, split * GROUP), pl.ds(split * GROUP, (groups - split) * GROUP)]
+    parts = [pl.ds(0, cut), pl.ds(cut, sent - cut)]
     mixed_copies = [
         [
             remote(
@@ -195,10 +219,14 @@
 
     def bias_group(j):
         chol_copy(j).wait()
-        block_rows = mixbuf[:, :, pl.ds(pl.multiple_of(j * GROUP, GROUP), GROUP), :]
-        density = jnp.dot(
-            block_rows.reshape(wide, electrons), trial[...], preferred_element_type=F32
-        ).astype(BF16)
+        first, tail, second = places[j]
+        block_rows = mixbuf[:, :, first : first + GROUP, :].reshape(wide, width)
+        if packed:
+            ends = mixbuf[:, :, tail : tail + GROUP, :].reshape(wide, width)
+            half = electrons - width
+            ends = ends[:, half:] if second else ends[:, :half]
+            block_rows = jnp.concatenate([block_rows, ends], axis=1)
+        density = jnp.dot(block_rows, trial[...], preferred_element_type=F32).astype(BF16)
 
         @pl.loop(0, deep // tile)
         def _(t):
@@ -210,12 +238,14 @@
     for copy in across_copies[0]:
         copy.wait_recv()
     loads[3].wait()
-    pl.loop(0, split - 1)(bias_group)
+    for j in range(split - 1):
+        bias_group(j)
     pass_across(1)
-    pl.loop(split - 1, split)(bias_group)
+    bias_group(split - 1)
     for copy in across_copies[1]:
         copy.wait_recv()
-    pl.loop(split, groups)(bias_group)
+    for j in range(split, groups):
+        bias_group(j)
 
     same = (
         lax.broadcasted_iota(jnp.int32, (1, GROUP, wide), 1)
@@ -325,7 +355,7 @@
         product = jnp.dot(
             pot[...].reshape(n * padded, orbitals), term, preferred_element_type=F32
         )
-        term = (product / jnp.float32(degree)).astype(BF16)
+        term = (product * jnp.float32(1.0 / degree)).astype(BF16)
         if padded != rows:
             term = jnp.dot(layout, term, preferred_element_type=F32).astype(BF16)
         summed = summed + term.astype(F32)
@@ -371,6 +401,7 @@
     span = groups * GROUP
     padded = span * ways
     walks = walk_count * every
+    _, _, sent, _, width = mixed_rows(groups, electrons)
     wide, deep = walks * GROUP, count * GROUP
     if padded != rows:
         cholesky = jnp.pad(cholesky, ((0, 0), (0, padded - rows), (0, 0)))
@@ -390,8 +421,8 @@
         scratch_shapes=[
             pltpu.VMEM((groups, count, GROUP, orbitals), BF16),
             pltpu.VMEM((2, half, orbitals), BF16),
-            pltpu.VMEM((n, ways, span, electrons), BF16),
-            pltpu.VMEM((2, every, span, electrons), BF16),
+            pltpu.VMEM((n, ways, sent, width), BF16),
+            pltpu.VMEM((2, every, sent, width), BF16),
             pltpu.VMEM((walk_count * n, half, orbitals), BF16),
             pltpu.VMEM((2, every, GROUP, LANES), BF16),
             pltpu.VMEM((deep, wide), F32),

time: 63.7 us -> 62.5 us (0.981)
  Pallas kernels: 60 us -> 58.8 us
    pallas_call x1, Pallas kernels: 60 us -> 58.8 us  [shards(): pl.pallas_call(functools.partial(step_kernel, n, ways, rows), out_shape=(...]
where the time goes in v6:
time: 62.5 us; the launch traced here: 62.4 us
  Pallas kernels  58.8 us (94%)
  local copies, waits for them, and re-layouts  2.88 us (5%)
  between operations  0.64 us (1%)
    pallas_call x1, Pallas kernels, shards(): pl.pallas_call(functools.partial(step_kernel, n, ways, rows), out_shape=(...  58.8 us
    unnamed x2, local copies, waits for them, and re-layouts  2.88 us

profile of v6, /device:TPU:0, one launch (start us, length us, event | category | flops | bytes accessed | tf_op | source)
XLA Modules:
  0.0 62.4 jit_solution(2481838802839110593)
XLA Ops:
  0.6 58.8 %shard_map.86 = (bf16[2,96,640]{2,1,0:T(8,128)(2,1)}, f32[2,128]{1,0:T(2,128)}) custom-call(bf16[128,160,640]{2,1,0:T(8,128)(2,1)} %chol.1, bf16[192,640]{1,0:T(8,128)(2,1)} %bitcast.5, bf16[2,192,192]{2,1,0:T(8,128)(2,1)} %inverse_in.1, bf16[2,96,640]{2,1,0:T(8,128)(2,1)} %bitcast.6, f32[8,128]{1,0:T(8,128)} %bitcast.7, s32[16]{0:T(128)} %offsets.1, s32[2]{0:T(128)} %parents.1), custom_call_target="tpu_custom_call" | custom-call | tf_op jit(solution)/shard_map/pallas_call | solution.py:413
  59.5 1.7 %copy.11 = bf16[2,640,96]{1,2,0:T(8,128)(2,1)} copy(bf16[2,640,96]{1,2,0:T(8,128)(2,1)} %bitcast.4) | data formatting | bytes 491520
  61.1 1.2 %copy.12 = f32[2,128]{1,0:T(2,128)} copy(f32[2,128]{1,0:T(2,128)} %get-tuple-element.9) | data formatting | bytes 2048

commit v7 on v6

--- a/solution.py
+++ b/solution.py
@@ -36,7 +36,7 @@
     n, ways, rows, chol, trial_in, inverse_in, walkers_in, noise_in, offsets, parents,
     walkers_out, bias_out,
     cbuf, wfirst, mixed, mixbuf, wbuf, rbuf, ybuf, ebuf, fbsend, fbbuf, fpad, kron, tmp, keep, psend, precv,
-    pfin, pot, xbuf, xsend, done, picks, window, trial, inverse, noise,
+    pfin, pot, xbuf, xsend, done, picks, window, trial, inverse, noise, biasbuf,
     csem, ssem, msem, xsem, hsem, rsem, fsem, qsem, psem, isem,
 ):
     a = lax.axis_index("pair")
@@ -328,7 +328,9 @@
     fbsend_rows = fpad.at[0:walks]
     fbsend_rows[...] = total
     for k in range(2):
-        bias_out[k : k + 1, :] = fpad[pl.ds(k * every + me, 1), :]
+        biasbuf[k : k + 1, :] = fpad[pl.ds(k * every + me, 1), :]
+    bias_copy = pltpu.make_async_copy(biasbuf, bias_out, isem.at[4])
+    bias_copy.start()
 
     for t in range(3, n):
         chain_step(t)
@@ -364,7 +366,8 @@
     ).astype(BF16).reshape(done.shape)
     last_copy = remote(done.at[1 - s], walkers_out.at[s], ssem, (2,), sibling)
     last_copy.start()
-    walkers_out[s] = done[s]
+    kept_copy = pltpu.make_async_copy(done.at[s], walkers_out.at[s], isem.at[5])
+    kept_copy.start()
 
     first_copy.wait_send()
     child_copy.wait_send()
@@ -384,7 +387,14 @@
         for d, b in peers:
             pot_copy(d, b, j).wait_send()
 
+    bias_copy.wait()
+    kept_copy.wait()
     last_copy.wait()
+
+
+def hand_over(walkers, bias, walkers_out, bias_out):
+    walkers_out[...] = walkers[...]
+    bias_out[...] = bias[...]
 
 
 def shards(cholesky, trial_orbitals, walkers, intersection_inverse, noise_stream, offsets, parents):
@@ -417,7 +427,7 @@
             jax.ShapeDtypeStruct((walk_count, count), F32),
         ),
         in_specs=[hbm, hbm, hbm, hbm, hbm, smem, smem],
-        out_specs=(vmem, vmem),
+        out_specs=(hbm, hbm),
         scratch_shapes=[
             pltpu.VMEM((groups, count, GROUP, orbitals), BF16),
             pltpu.VMEM((2, half, orbitals), BF16),
@@ -445,6 +455,7 @@
             pltpu.VMEM((electrons, orbitals), BF16),
             pltpu.VMEM((walk_count, electrons, electrons), BF16),
             pltpu.VMEM((noise_stream.shape[0] // LANES, LANES), F32),
+            pltpu.VMEM((walk_count, count), F32),
             dma((groups,)),
             dma((2, 3)),
             dma((2, 2, every)),
@@ -454,7 +465,7 @@
             dma((2, every)),
             dma((2, groups)),
             dma((2, every, groups)),
-            dma((4,)),
+            dma((6,)),
         ],
         compiler_params=pltpu.CompilerParams(
             collective_id=0, has_side_effects=True, vmem_limit_bytes=58 * 1024 * 1024
@@ -463,6 +474,16 @@
         cholesky, trial_orbitals.T, intersection_inverse, jnp.swapaxes(walkers, 1, 2),
         noise_stream.reshape(-1, LANES), offsets, parents,
     )
+    new_walkers, force_bias = pl.pallas_call(
+        hand_over,
+        out_shape=(
+            jax.ShapeDtypeStruct(new_walkers.shape, BF16),
+            jax.ShapeDtypeStruct(force_bias.shape, F32),
+        ),
+        in_specs=[vmem, vmem],
+        out_specs=(vmem, vmem),
+        compiler_params=pltpu.CompilerParams(vmem_limit_bytes=58 * 1024 * 1024),
+    )(new_walkers, force_bias)
     return (jnp.swapaxes(new_walkers, 1, 2), force_bias)
 
 

time: 62.5 us -> 60.8 us (0.973)
  local copies, waits for them, and re-layouts: 2.88 us -> 0 us
  Pallas kernels: 58.8 us -> 59.9 us
    unnamed x2 -> x0, local copies, waits for them, and re-layouts: 2.88 us -> none
    pallas_call x0 -> x1, Pallas kernels: none -> 1.66 us  [shards(): pl.pallas_call(hand_over, out_shape=(jax.ShapeDtypeStruct(new_walkers.sha...]
where the time goes in v7:
time: 60.8 us; the launch traced here: 60.6 us
  Pallas kernels  59.9 us (99%)
  between operations  0.64 us (1%)
    pallas_call x1, Pallas kernels, shards(): pl.pallas_call(functools.partial(step_kernel, n, ways, rows), out_shape=(...  58.3 us
    pallas_call x1, Pallas kernels, shards(): pl.pallas_call(hand_over, out_shape=(jax.ShapeDtypeStruct(new_walkers.sha...  1.66 us

profile of v7, /device:TPU:0, one launch (start us, length us, event | category | flops | bytes accessed | tf_op | source)
XLA Modules:
  0.0 60.6 jit_solution(4469982736344158654)
XLA Ops:
  0.6 58.3 %shard_map.86 = (bf16[2,96,640]{2,1,0:T(8,128)(2,1)}, f32[2,128]{1,0:T(2,128)}) custom-call(bf16[128,160,640]{2,1,0:T(8,128)(2,1)} %chol.1, bf16[192,640]{1,0:T(8,128)(2,1)} %bitcast.4, bf16[2,192,192]{2,1,0:T(8,128)(2,1)} %inverse_in.1, bf16[2,96,640]{2,1,0:T(8,128)(2,1)} %bitcast.5, f32[8,128]{1,0:T(8,128)} %bitcast.6, s32[16]{0:T(128)} %offsets.1, s32[2]{0:T(128)} %parents.1), custom_call_target="tpu_custom_call" | custom-call | tf_op jit(solution)/shard_map/pallas_call | solution.py:423
  58.9 1.7 %shard_map.87 = (bf16[2,96,640]{2,1,0:T(8,128)(2,1)}, f32[2,128]{1,0:T(2,128)}) custom-call(bf16[2,96,640]{2,1,0:T(8,128)(2,1)} %get-tuple-element.6.walkers, f32[2,128]{1,0:T(2,128)} %get-tuple-element.7.bias), custom_call_target="tpu_custom_call" | custom-call | tf_op jit(solution)/shard_map/pallas_call | solution.py:477

commit v8 on v7

--- a/solution.py
+++ b/solution.py
@@ -264,9 +264,9 @@
     bias_copies = [remote(fbsend, fbbuf.at[me], fsem, (d,), holder(c)) for d, c in peers]
     for copy in bias_copies:
         copy.start()
-    chain_step(1)
     for copy in pick_copies + bias_copies:
         copy.wait_recv()
+    chain_step(1)
     total = jnp.sum(fbbuf[...], axis=0)
     fpad[0:walks, :] = window[:, 0:LANES] - total
     fields = fpad[...].astype(BF16)

time: 60.8 us -> 62.2 us (1.023)
  Pallas kernels: 59.9 us -> 61.4 us
    pallas_call x1, Pallas kernels: 58.3 us -> 59.8 us  [shards(): pl.pallas_call(functools.partial(step_kernel, n, ways, rows), out_shape=(...]
where the time goes in v8:
time: 62.2 us; the launch traced here: 62.1 us
  Pallas kernels  61.4 us (99%)
  between operations  0.64 us (1%)
    pallas_call x1, Pallas kernels, shards(): pl.pallas_call(functools.partial(step_kernel, n, ways, rows), out_shape=(...  59.8 us
    pallas_call x1, Pallas kernels, shards(): pl.pallas_call(hand_over, out_shape=(jax.ShapeDtypeStruct(new_walkers.sha...  1.66 us

profile of v8, /device:TPU:0, one launch (start us, length us, event | category | flops | bytes accessed | tf_op | source)
XLA Modules:
  0.0 62.1 jit_solution(13256199740134499165)
XLA Ops:
  0.6 59.8 %shard_map.86 = (bf16[2,96,640]{2,1,0:T(8,128)(2,1)}, f32[2,128]{1,0:T(2,128)}) custom-call(bf16[128,160,640]{2,1,0:T(8,128)(2,1)} %chol.1, bf16[192,640]{1,0:T(8,128)(2,1)} %bitcast.4, bf16[2,192,192]{2,1,0:T(8,128)(2,1)} %inverse_in.1, bf16[2,96,640]{2,1,0:T(8,128)(2,1)} %bitcast.5, f32[8,128]{1,0:T(8,128)} %bitcast.6, s32[16]{0:T(128)} %offsets.1, s32[2]{0:T(128)} %parents.1), custom_call_target="tpu_custom_call" | custom-call | tf_op jit(solution)/shard_map/pallas_call | solution.py:423
  60.4 1.7 %shard_map.87 = (bf16[2,96,640]{2,1,0:T(8,128)(2,1)}, f32[2,128]{1,0:T(2,128)}) custom-call(bf16[2,96,640]{2,1,0:T(8,128)(2,1)} %get-tuple-element.6.walkers, f32[2,128]{1,0:T(2,128)} %get-tuple-element.7.bias), custom_call_target="tpu_custom_call" | custom-call | tf_op jit(solution)/shard_map/pallas_call | solution.py:477
